TPU v7x, 512 devices: a whole 4x4x16 slice. The times are simulated.
512 devices in a mesh: row: 16 (over x, z_hi), col: 4 (over z_lo), depth: 8 (over y, core).
Axes of the slice: x: 4, y: 4, z: 16 (z_hi: 4, z_lo: 4; z = z_hi * 4 + z_lo), core: 2. Of those that a mesh axis runs over, the one named last changes fastest.
Arguments:
- features: bfloat16 [256, 16384], P('depth', ('col', 'row')), may hold values from -6 to 6
- weight: bfloat16 [256, 172], P('depth'), may hold values from -1.25 to 1.25
- tile_values: bfloat16 [8192, 128, 128], P(('row', 'col')), may hold values from -0.109375 to 0.109375
- tile_rows: int32 [8192], P(('row', 'col')), may hold values from 0 to 7
- tile_cols: int32 [8192], P(('row', 'col')), may hold values from 0 to 31
- tile_count: int32 [64], P(('row', 'col')), may hold values from 1 to 128, as said below
- labels: int32 [16384], P(('row', 'col')), may hold values from 0 to 171
Outputs:
- weight_grad: float32 [256, 172], P('depth')
- feature_grad: float32 [256, 16384], P('depth', ('col', 'row'))
Inputs may be any that keep to these rules, and one draw needn't show every extreme that they name: `tile_rows`: tile positions may repeat within a device; repeated tiles add. `tile_count`: some device has all 128 slots live.
All inputs are finite; a program needn't handle non-finite values.
Results may differ from a plain program's by a relative error of at most 0.019.
Values may be sent and summed in bfloat16 or wider, within the bound.
No kernel may reach another device: no remote copies, remote signals or barrier semaphores. Data moves between devices by JAX's collectives and lax.ppermute only.
A program may use at most 64 MiB of HBM per device.

v0:
```python
import jax
import jax.numpy as jnp
from jax import lax
from jax.sharding import PartitionSpec as P

TILE = 128


def class_delta(logits, labels):
    exponent = jnp.exp(logits)
    chances = exponent / jnp.sum(exponent, axis=0, keepdims=True)
    target = (lax.broadcasted_iota(jnp.int32, logits.shape, 0) == labels[None, :]).astype(
        jnp.float32
    )
    return (chances - target).astype(jnp.bfloat16)


def tile_products(source, tile_values, pick_index, put_index, live_count, put_tiles, backward):
    hidden = source.shape[0]
    slot_total = tile_values.shape[0]
    picked = jnp.take(source, pick_index, axis=1)
    if backward:
        products = jnp.einsum(
            "hki,kij->hkj", picked, tile_values, preferred_element_type=jnp.float32
        )
    else:
        products = jnp.einsum(
            "hkj,kij->hki", picked, tile_values, preferred_element_type=jnp.float32
        )
    slot_ids = jnp.arange(slot_total, dtype=jnp.int32)
    live_mask = slot_ids < live_count
    placing = (
        (put_index[:, None] == jnp.arange(put_tiles, dtype=jnp.int32)[None, :]) & live_mask[:, None]
    ).astype(jnp.float32)
    running = jnp.einsum("hkt,kp->hpt", products, placing)
    return running.reshape(hidden, put_tiles * TILE)


def body(features, weight, tile_values, tile_rows, tile_cols, tile_count, labels):
    hidden = features.shape[0]
    node_count = features.shape[1]
    live_count = tile_count[0]
    gathered = lax.all_gather(features, "row", axis=1, tiled=True)
    col_tiles = gathered.shape[1] // TILE
    row_tiles = lax.axis_size("col") * node_count // TILE
    source = gathered.reshape(hidden, col_tiles, TILE)
    partial_value = tile_products(
        source, tile_values, tile_cols, tile_rows, live_count, row_tiles, False
    )
    whole_sum = lax.psum(partial_value, "col")
    summed = lax.dynamic_slice_in_dim(whole_sum, lax.axis_index("col") * node_count, node_count, 1)
    aggregated = summed.astype(jnp.bfloat16)
    logit_part = lax.dot_general(
        weight, aggregated, (((0,), (0,)), ((), ())), preferred_element_type=jnp.float32
    )
    logits = lax.psum(logit_part, "depth")
    delta = class_delta(logits, labels)
    weight_term = lax.dot_general(
        aggregated, delta, (((1,), (1,)), ((), ())), preferred_element_type=jnp.float32
    )
    weight_grad = lax.psum(weight_term, ("row", "col"))
    grad_hidden = jnp.dot(weight, delta, preferred_element_type=jnp.float32).astype(jnp.bfloat16)
    grad_rows = lax.all_gather(grad_hidden, "col", axis=1, tiled=True)
    back_source = grad_rows.reshape(hidden, row_tiles, TILE)
    back_partial = tile_products(
        back_source, tile_values, tile_rows, tile_cols, live_count, col_tiles, True
    )
    whole_back = lax.psum(back_partial, "row")
    feature_grad = lax.dynamic_slice_in_dim(
        whole_back, lax.axis_index("row") * node_count, node_count, 1
    )
    return (weight_grad, feature_grad)


def solution(mesh):
    return jax.shard_map(
        body,
        mesh=mesh,
        in_specs=(
            P("depth", ("col", "row")),
            P("depth", None),
            P(("row", "col"), None, None),
            P(("row", "col")),
            P(("row", "col")),
            P(("row", "col")),
            P(("row", "col")),
        ),
        out_specs=(P("depth", None), P("depth", ("col", "row"))),
        check_vma=False,
    )
```

profile of v0, /device:TPU:8, one launch (start us, length us, event | category | flops | bytes accessed | tf_op | source)
XLA Modules:
  0.0 470.4 jit_solution(2844313566533550606)
XLA Ops:
  7.2 0.0 copy-start
  7.2 0.0 all-reduce.4.cloned.1.call-start
  7.2 0.7 compare_and_fusion.1
  7.9 0.7 compare_select_fusion.1
  9.2 60.6 %all_gather.6 = bf16[32,4096]{1,0:T(8,128)(2,1)S(1)} all-gather(bf16[32,256]{1,0:T(8,128)(2,1)} %param.7), channel_id=1, replica_groups=mesh['row'=16,'col'=4,'depth'=8] {'row'}, dimensions={1}, use_global_device_ids=true | all-gather | bytes 278528 | tf_op jit(solution)/shard_map/all_gather | solution.py:43
  69.9 0.0 copy-start.2
  69.9 0.8 gather_fusion
  70.7 0.0 copy-start.1
  70.7 4.5 convolution_bitcast_fusion.1
  75.2 0.0 copy-done.2
  75.2 0.4 fusion.2
  75.6 19.6 %all-reduce.7 = bf16[32,1024]{1,0:T(8,128)(2,1)S(1)} all-reduce(f32[32,1024]{1,0:T(8,128)S(1)} %bitcast.50), channel_id=1, replica_groups=mesh['row'=16,'col'=4,'depth'=8] {'col'}, use_global_device_ids=true, to_apply=%region_0.1 | all-reduce | flops 32768 | bytes 196608 | tf_op jit(solution)/shard_map/psum | solution.py:50
  95.2 0.0 copy-done
  95.2 0.9 convolution_bitcast_fusion.2
  96.2 0.0 all-reduce.4.cloned.1.call-update
  96.2 0.0 all-reduce.6.cloned.1.call-start
  96.3 64.1 %all-reduce.4.cloned.1.call-done = f32[172,256]{1,0:T(8,128)} async-done(((f32[172,256]{1,0:T(8,128)}), f32[172,256]{1,0:T(8,128)}) %all-reduce.4.cloned.1.call-update) | async-done | bytes 176144 | tf_op jit(solution)/shard_map/psum | solution.py:56
  160.4 1.0 exponential_reduce_fusion
  161.4 0.0 copy-done.1
  161.4 1.0 subtract_convert_fusion
  162.3 0.1 fusion.4
  162.5 13.5 %all_gather.7 = bf16[32,1024]{1,0:T(8,128)(2,1)S(1)} all-gather(bf16[32,256]{1,0:T(8,128)(2,1)S(1)} %fusion.4), channel_id=1, replica_groups=mesh['row'=16,'col'=4,'depth'=8] {'col'}, dimensions={1}, use_global_device_ids=true | all-gather | bytes 81920 | tf_op jit(solution)/shard_map/all_gather | solution.py:63
  175.9 0.0 copy-start.3
  176.0 0.8 gather_fusion.1
  176.7 3.4 convolution_bitcast_fusion
  180.2 0.0 copy-done.3
  180.2 0.4 fusion
  180.6 1.1 copy.26
  181.7 0.0 all-reduce.6.cloned.1.call-update
  181.8 0.1 fusion.18
  181.9 280.3 %psum.30 = f32[32,172]{1,0:T(8,128)} all-reduce(f32[32,172]{1,0:T(8,128)S(1)} %fusion.18), channel_id=1, replica_groups=mesh['row'=16,'col'=4,'depth'=8] {'row','col'}, use_global_device_ids=true, to_apply=%region_3.4 | all-reduce | flops 5504 | bytes 44032 | tf_op jit(solution)/shard_map/psum | solution.py:61
  462.2 1.4 constant_dynamic-slice_fusion
  (9 shorter events, 0.1 us)
Async XLA Ops:
  7.2 88.1 %copy-start = (bf16[32,172]{1,0:T(8,128)(2,1)S(1)}, bf16[32,172]{1,0:T(8,128)(2,1)}, u32[]{:S(2)}) copy-start(bf16[32,172]{1,0:T(8,128)(2,1)} %param.8) | copy-start | bytes 33028
  7.2 153.2 %all-reduce.4.cloned.1.call-start = ((), (), s32[]{:S(2)}) async-start(), calls=%async_computation | async-start | bytes 360448 | tf_op jit(solution)/shard_map/psum | solution.py:56
  69.9 5.3 %copy-start.2 = (s32[128]{0:T(128)S(1)}, s32[128]{0:T(128)}, u32[]{:S(2)}) copy-start(s32[128]{0:T(128)} %param.10) | copy-start | bytes 1540
  70.7 90.7 %copy-start.1 = (s32[256]{0:T(256)S(1)}, s32[256]{0:T(256)}, u32[]{:S(2)}) copy-start(s32[256]{0:T(256)} %param.13) | copy-start | bytes 3076
  96.2 366.0 %all-reduce.6.cloned.1.call-start = ((), (), s32[]{:S(2)}) async-start(), calls=%async_computation.1 | async-start | bytes 1048576 | tf_op jit(solution)/shard_map/psum | solution.py:68
  175.9 4.2 copy-start.3
Sparse Core Ops, SparseCore 0:
  96.3 64.0 all-reduce.3
  181.9 208.7 all-reduce.5
where the time goes:
time: 471 us; the launch traced here: 470 us
  blocking collectives  374 us (79%)
  waiting for transfers between devices  64.2 us (14%)
  between operations  14.8 us (3%)
  matrix products  9.97 us (2%)
    psum x1, blocking collectives, body(): weight_grad = lax.psum(weight_term, ('row', 'col'))  280 us
    psum x1, waiting for transfers between devices, body(): logits = lax.psum(logit_part, 'depth')  64.1 us
    all_gather x1, blocking collectives, body(): gathered = lax.all_gather(features, 'row', axis=1, tiled=True)  60.6 us
    psum x1, blocking collectives, body(): whole_sum = lax.psum(partial_value, 'col')  19.6 us
    all_gather x1, blocking collectives, body(): grad_rows = lax.all_gather(grad_hidden, 'col', axis=1, tiled=True)  13.5 us
  transfers between devices with their start and end apart: 2, of which 1 were waited for; matrix products, arithmetic and copies ran while one was open for 0% of the time, Pallas kernels for 0%

commit v1 on v0

v1 whole, which is shorter than its diff:
```python
import jax
import jax.numpy as jnp
from jax import lax
from jax.experimental import pallas as pl
from jax.experimental.pallas import tpu as pltpu
from jax.sharding import Mesh
from jax.sharding import PartitionSpec as P

TILE = 128
STEP = 16
AXES = ("x", "zh", "zl", "y", "core")
ROW = ("x", "zh")
DEPTH = ("y", "core")
SMEM = pltpu.MemorySpace.SMEM
F32 = jnp.float32
BF16 = jnp.bfloat16
NT = (((1,), (1,)), ((), ()))
TN = (((0,), (0,)), ((), ()))


def forward_kernel(count_ref, rows_ref, cols_ref, where_ref, source_ref, weight_ref, labels_ref, tiles_ref, out_ref, total):
    step = pl.program_id(0)
    blocks = total.shape[0] - 1

    @pl.when(step == 0)
    def clear():
        total[...] = jnp.zeros_like(total)

    live = count_ref[0]
    products = []
    for j in range(STEP):
        col = cols_ref[step * STEP + j]
        lanes = pl.ds(pl.multiple_of((col % 2) * TILE, TILE), TILE)
        products.append(
            lax.dot_general(source_ref[col // 2, :, lanes], tiles_ref[j], NT, preferred_element_type=F32)
        )
    for j in range(STEP):
        slot = step * STEP + j
        row = jnp.where(slot < live, rows_ref[slot], blocks)
        total[row] = total[row] + products[j]

    @pl.when(step == pl.num_programs(0) - 1)
    def finish():
        me = where_ref[0]
        weight = weight_ref[...].astype(F32)
        classes = weight.shape[1]
        mine = weight[0:8]
        for z in range(1, 4):
            mine = jnp.where(me == z, weight[8 * z : 8 * z + 8], mine)
        labels = labels_ref[...].astype(F32)
        left = mine[:, :TILE]
        rest = jnp.concatenate([mine[:, TILE:], jnp.zeros((8, 64 - (classes - TILE)), F32)], axis=1)
        for d in range(blocks):
            out_ref[0, d, 0:32, :] = total[d].astype(BF16)
            half = labels[:, (d % 2) * TILE : (d % 2) * TILE + TILE]
            both = jnp.concatenate([half[:, :64], half[:, 64:], jnp.zeros((6, 64), F32)], axis=0)
            right = jnp.concatenate([rest, both], axis=1)
            out_ref[0, d, 32:48, :] = jnp.concatenate([left, right], axis=0).astype(BF16)
        for z in range(1, 4):
            out_ref[z] = out_ref[0]


def middle_kernel(where_ref, got_ref, out_ref, agg, weight_a, weight_b):
    me = where_ref[1]
    for d in range(8):
        sums = got_ref[d, 0:32, :].astype(F32)
        for z in range(1, 4):
            sums = sums + got_ref[8 * z + d, 0:32, :].astype(F32)
        agg[32 * d : 32 * d + 32, :] = sums.astype(BF16)
        pieces = [got_ref[8 * z + d, 32:48, :].astype(F32) for z in range(4)]
        weight_a[32 * d : 32 * d + 32, :] = jnp.concatenate([p[0:8] for p in pieces], axis=0).astype(BF16)
        weight_b[32 * d : 32 * d + 32, :] = jnp.concatenate([p[8:16] for p in pieces], axis=0).astype(BF16)
    carrier = got_ref[(me // 2) * 8, 32:48, :].astype(F32)
    labels = jnp.concatenate([carrier[8:9, 64:], carrier[9:10, 64:]], axis=1)
    nodes = agg[...]
    wa = weight_a[...]
    wb = weight_b[...]
    ids = lax.broadcasted_iota(jnp.int32, (TILE, TILE), 0).astype(F32)
    exp_a = jnp.exp(lax.dot_general(wa, nodes, TN, preferred_element_type=F32))
    logit_b = lax.dot_general(wb, nodes, TN, preferred_element_type=F32)
    valid = ids < 172 - TILE
    exp_b = jnp.where(valid, jnp.exp(jnp.where(valid, logit_b, 0.0)), 0.0)
    whole = jnp.sum(exp_a, axis=0, keepdims=True) + jnp.sum(exp_b, axis=0, keepdims=True)
    delta_a = (exp_a / whole - jnp.where(ids == labels, 1.0, 0.0)).astype(BF16)
    delta_b = (exp_b / whole - jnp.where(ids + TILE == labels, 1.0, 0.0)).astype(BF16)
    hidden = jnp.dot(wa, delta_a, preferred_element_type=F32) + jnp.dot(wb, delta_b, preferred_element_type=F32)
    grad_a = lax.dot_general(nodes, delta_a, NT, preferred_element_type=F32)
    grad_b = lax.dot_general(nodes, delta_b, NT, preferred_element_type=F32)
    for d in range(8):
        out_ref[d, 0:32, :] = hidden[32 * d : 32 * d + 32].astype(BF16)
        out_ref[d, 32:64, :] = grad_a[32 * d : 32 * d + 32].astype(BF16)
        part = grad_b[32 * d : 32 * d + 32, :64]
        out_ref[d, 64:80, :] = jnp.concatenate([part[0:16], part[16:32]], axis=1).astype(BF16)


def backward_kernel(count_ref, rows_ref, cols_ref, got_ref, tiles_ref, out_ref, total):
    step = pl.program_id(0)
    blocks = total.shape[0] - 1

    @pl.when(step == 0)
    def clear():
        total[...] = jnp.zeros_like(total)

    live = count_ref[0]
    products = []
    for j in range(STEP):
        row = rows_ref[step * STEP + j]
        products.append(jnp.dot(got_ref[row, 0:32, :], tiles_ref[j], preferred_element_type=F32))
    for j in range(STEP):
        slot = step * STEP + j
        col = jnp.where(slot < live, cols_ref[slot], blocks)
        total[col] = total[col] + products[j]

    @pl.when(step == pl.num_programs(0) - 1)
    def finish():
        grad_a = got_ref[0, 32:64, :].astype(F32)
        grad_b = got_ref[0, 64:80, :].astype(F32)
        for d in range(1, 8):
            grad_a = grad_a + got_ref[d, 32:64, :].astype(F32)
            grad_b = grad_b + got_ref[d, 64:80, :].astype(F32)
        for x in range(4):
            for z in range(4):
                for half in range(2):
                    out_ref[x, 32 * z : 32 * z + 32, half * TILE : half * TILE + TILE] = total[
                        (4 * x + z) * 2 + half
                    ].astype(BF16)
            out_ref[x, 128:144, 0:TILE] = grad_a[0:16].astype(BF16)
            out_ref[x, 128:144, TILE:] = grad_a[16:32].astype(BF16)
            out_ref[x, 144:160, 0:TILE] = grad_b.astype(BF16)
            out_ref[x, 144:160, TILE:] = jnp.zeros((16, TILE), BF16)


def sum_kernel(got_ref, out_ref):
    sums = got_ref[0].astype(F32)
    for x in range(1, 4):
        sums = sums + got_ref[x].astype(F32)
    out_ref[...] = sums.astype(BF16)


def final_kernel(where_ref, got_ref, weight_ref, feature_ref):
    at = pl.multiple_of(where_ref[2] * 32, 32)
    sums = got_ref[0, pl.ds(at, 32), :].astype(F32)
    grads = got_ref[0, 128:160, :].astype(F32)
    for z in range(1, 4):
        sums = sums + got_ref[z, pl.ds(at, 32), :].astype(F32)
        grads = grads + got_ref[z, 128:160, :].astype(F32)
    feature_ref[...] = sums
    weight_ref[0:16, 0:TILE] = grads[0:16, 0:TILE]
    weight_ref[16:32, 0:TILE] = grads[0:16, TILE:]
    weight_ref[0:16, TILE:] = grads[16:32, 0:44]
    weight_ref[16:32, TILE:] = grads[16:32, 64:108]


def tile_call(kernel, arrays, tiles, out_shape, blocks, smem):
    slots = tiles.shape[0]

    def whole(array):
        return pl.BlockSpec(array.shape, lambda i, n=len(array.shape): (0,) * n)

    return pl.pallas_call(
        kernel,
        grid=(slots // STEP,),
        in_specs=[pl.BlockSpec(memory_space=SMEM)] * smem
        + [whole(a) for a in arrays[smem:]]
        + [pl.BlockSpec((STEP, TILE, TILE), lambda i: (i, 0, 0))],
        out_specs=whole(out_shape),
        out_shape=out_shape,
        scratch_shapes=[pltpu.VMEM((blocks + 1, 32, TILE), F32)],
        compiler_params=pltpu.CompilerParams(vmem_limit_bytes=24 * 2**20),
    )(*arrays, tiles)


def body(features, weight, tile_values, tile_rows, tile_cols, tile_count, labels):
    shape = jax.ShapeDtypeStruct
    vmem = pl.BlockSpec(memory_space=pltpu.VMEM)
    scalars = pl.BlockSpec(memory_space=SMEM)
    where = jnp.stack([lax.axis_index("zl"), lax.axis_index(DEPTH), lax.axis_index("zh")]).astype(jnp.int32)
    near = lax.all_gather(features, "zh", axis=0)
    source = lax.all_gather(near, "x", axis=0).reshape(16, 32, 256)
    sent = tile_call(
        forward_kernel,
        [tile_count, tile_rows, tile_cols, where, source, weight, labels.reshape(1, 256)],
        tile_values,
        shape((4, 8, 48, TILE), BF16),
        8,
        4,
    )
    got = lax.all_to_all(sent.reshape(32, 48, TILE), ("zl", "y", "core"), 0, 0, tiled=True)
    back = pl.pallas_call(
        middle_kernel,
        in_specs=[scalars, vmem],
        out_specs=vmem,
        out_shape=shape((8, 80, TILE), BF16),
        scratch_shapes=[pltpu.VMEM((256, TILE), BF16)] * 3,
    )(where, got)
    grads = lax.all_to_all(back, DEPTH, 0, 0, tiled=True)
    parts = tile_call(
        backward_kernel,
        [tile_count, tile_rows, tile_cols, grads],
        tile_values,
        shape((4, 160, 256), BF16),
        32,
        3,
    )
    ours = lax.all_to_all(parts, "x", 0, 0, tiled=True)
    summed = pl.pallas_call(
        sum_kernel, in_specs=[vmem], out_specs=vmem, out_shape=shape((160, 256), BF16)
    )(ours)
    four = lax.all_gather(summed, "zh", axis=0)
    return pl.pallas_call(
        final_kernel,
        in_specs=[scalars, vmem],
        out_specs=(vmem, vmem),
        out_shape=(shape((32, 172), F32), shape((32, 256), F32)),
    )(where, four)


def solution(mesh):
    fine = Mesh(mesh.devices.reshape(4, 4, 4, 4, 2), AXES)
    tiled = ("x", "zh", "zl")
    return jax.shard_map(
        body,
        mesh=fine,
        in_specs=(
            P(DEPTH, ("zl", "x", "zh")),
            P(DEPTH, None),
            P(tiled, None, None),
            P(tiled),
            P(tiled),
            P(tiled),
            P(tiled),
        ),
        out_specs=(P(DEPTH, None), P(DEPTH, ("zl", "x", "zh"))),
        check_vma=False,
    )
```

time: 471 us -> 121 us (0.26)
  the two profiles are of different devices: /device:TPU:8 before, /device:TPU:32 now
where the time goes in v1:
time: 121 us; the launch traced here: 120 us
  blocking collectives  99.2 us (82%)
  Pallas kernels  12.3 us (10%)
  local copies, waits for them, and re-layouts  7.1 us (6%)
  between operations  1.34 us (1%)
    all_gather x1, blocking collectives, body(): near = lax.all_gather(features, 'zh', axis=0)  25 us
    all_gather x1, blocking collectives, body(): four = lax.all_gather(summed, 'zh', axis=0)  21.5 us
    all_to_all x1, blocking collectives, body(): lax.all_to_all(sent.reshape(32, 48, TILE), ('zl', 'y', 'core'), 0, 0, til...  19.6 us
    all_gather x1, blocking collectives, body(): source = lax.all_gather(near, 'x', axis=0).reshape(16, 32, 256)  12.6 us
    all_to_all x1, blocking collectives, body(): ours = lax.all_to_all(parts, 'x', 0, 0, tiled=True)  10.7 us
    all_to_all x1, blocking collectives, body(): grads = lax.all_to_all(back, DEPTH, 0, 0, tiled=True)  9.77 us
    unnamed x18, local copies, waits for them, and re-layouts  7.1 us
    pallas_call x2, Pallas kernels, tile_call(): pl.pallas_call(kernel, grid=(slots // STEP,), in_specs=[pl.BlockSpec(memo...  6.74 us

profile of v1, /device:TPU:32, one launch (start us, length us, event | category | flops | bytes accessed | tf_op | source)
XLA Modules:
  0.0 120.1 jit_solution(17758503137009697297)
XLA Ops:
  0.6 0.0 copy-start.7
  0.6 0.0 copy-start.5
  1.3 25.0 %all-gather = bf16[128,256]{1,0:T(8,128)(2,1)S(1)} all-gather(bf16[32,256]{1,0:T(8,128)(2,1)} %param.7), channel_id=2, replica_groups=mesh['x'=4,'zh'=4,'zl'=4,'y'=4,'core'=2] {'zh'}, dimensions={0}, use_global_device_ids=true | all-gather | bytes 81920 | tf_op jit(solution)/shard_map/all_gather | solution.py:178
  26.3 12.6 %all-gather.1.source_ref = bf16[16,32,256]{2,1,0:T(8,128)(2,1)S(1)} all-gather(bf16[4,32,256]{2,1,0:T(8,128)(2,1)S(1)} %bitcast.10), channel_id=3, replica_groups=mesh['x'=4,'zh'=4,'zl'=4,'y'=4,'core'=2] {'x'}, dimensions={0}, use_global_device_ids=true | all-gather | bytes 327680 | tf_op jit(solution)/shard_map/all_gather | solution.py:179
  38.9 0.1 pad_add_fusion.where_ref
  39.0 0.0 copy-start.3
  39.0 0.0 copy-start
  39.0 2.2 %copy-done = bf16[128,128,128]{2,1,0:T(8,128)(2,1)S(1)} copy-done((bf16[128,128,128]{2,1,0:T(8,128)(2,1)S(1)}, bf16[128,128,128]{2,1,0:T(8,128)(2,1)}, u32[]{:S(2)}) %copy-start) | copy-done | bytes 4194328
  41.2 0.0 copy-start.2
  41.2 0.7 copy-done.2
  41.9 0.0 copy-start.4
  41.9 0.7 copy-done.4
  42.6 0.0 copy-start.6
  42.6 0.7 copy-done.6
  43.2 0.0 copy-start.8
  43.2 0.7 copy-done.8
  43.9 3.9 %shard_map.86 = bf16[4,8,48,128]{3,2,1,0:T(8,128)(2,1)S(1)} custom-call(s32[1]{0:T(128)S(6)} %copy.9.count_ref, s32[128]{0:T(128)S(1)} %copy-done.4, s32[128]{0:T(128)S(1)} %copy-done.6, s32[3]{0:T(128)S(1)} %pad_add_fusion.where_ref, bf16[16,32,256]{2,1,0:T(8,128)(2,1)S(1)} %all-gather.1.source_ref, bf16[32,172]{1,0:T(8,128)(2,1)S(1)} %copy-done.2, ...), custom_call_target="tpu_custom_call" | custom-call | tf_op jit(solution)/shard_map/pallas_call | solution.py:160
  47.8 19.6 %all_to_all.15.got_ref = bf16[32,48,128]{2,1,0:T(8,128)(2,1)} all-to-all(bf16[32,48,128]{2,1,0:T(8,128)(2,1)S(1)} %bitcast.7), channel_id=1, replica_groups=mesh['x'=4,'zh'=4,'zl'=4,'y'=4,'core'=2] {'zl','y','core'}, dimensions={0} | all-to-all | bytes 786432 | tf_op jit(solution)/shard_map/all_to_all | solution.py:188
  67.5 0.0 copy-done.3
  67.5 2.2 %shard_map.87 = bf16[8,80,128]{2,1,0:T(8,128)(2,1)} custom-call(s32[3]{0:T(128)} %copy-done.3, bf16[32,48,128]{2,1,0:T(8,128)(2,1)} %all_to_all.15.got_ref), custom_call_target="tpu_custom_call" | custom-call | tf_op jit(solution)/shard_map/pallas_call | solution.py:189
  69.7 9.8 %all_to_all.16.got_ref = bf16[8,80,128]{2,1,0:T(8,128)(2,1)S(1)} all-to-all(bf16[8,80,128]{2,1,0:T(8,128)(2,1)} %shard_map.87), channel_id=1, replica_groups=mesh['x'=4,'zh'=4,'zl'=4,'y'=4,'core'=2] {'y','core'}, dimensions={0} | all-to-all | bytes 327680 | tf_op jit(solution)/shard_map/all_to_all | solution.py:196
  79.5 0.0 copy-done.7
  79.5 0.0 copy-done.5
  79.5 0.0 copy-start.1
  79.5 2.2 %copy-done.1 = bf16[128,128,128]{2,1,0:T(8,128)(2,1)S(1)} copy-done((bf16[128,128,128]{2,1,0:T(8,128)(2,1)S(1)}, bf16[128,128,128]{2,1,0:T(8,128)(2,1)}, u32[]{:S(2)}) %copy-start.1) | copy-done | bytes 4194328
  81.7 2.8 %shard_map.88 = bf16[4,160,256]{2,1,0:T(8,128)(2,1)S(1)} custom-call(s32[1]{0:T(128)S(6)} %copy.9.count_ref, s32[128]{0:T(128)S(1)} %copy-done.5, s32[128]{0:T(128)S(1)} %copy-done.7, bf16[8,80,128]{2,1,0:T(8,128)(2,1)S(1)} %all_to_all.16.got_ref, bf16[128,128,128]{2,1,0:T(8,128)(2,1)S(1)} %copy-done.1), custom_call_target="tpu_custom_call" | custom-call | tf_op jit(solution)/shard_map/pallas_call | solution.py:160
  84.5 10.7 %all_to_all.17.got_ref = bf16[4,160,256]{2,1,0:T(8,128)(2,1)} all-to-all(bf16[4,160,256]{2,1,0:T(8,128)(2,1)S(1)} %shard_map.88), channel_id=1, replica_groups=mesh['x'=4,'zh'=4,'zl'=4,'y'=4,'core'=2] {'x'}, dimensions={0} | all-to-all | bytes 655360 | tf_op jit(solution)/shard_map/all_to_all | solution.py:205
  95.3 1.6 %shard_map.89 = bf16[160,256]{1,0:T(8,128)(2,1)} custom-call(bf16[4,160,256]{2,1,0:T(8,128)(2,1)} %all_to_all.17.got_ref), custom_call_target="tpu_custom_call" | custom-call | tf_op jit(solution)/shard_map/pallas_call | solution.py:206
  96.9 21.5 %all-gather.2 = bf16[640,256]{1,0:T(8,128)(2,1)} all-gather(bf16[160,256]{1,0:T(8,128)(2,1)} %shard_map.89), channel_id=4, replica_groups=mesh['x'=4,'zh'=4,'zl'=4,'y'=4,'core'=2] {'zh'}, dimensions={0}, use_global_device_ids=true | all-gather | bytes 409600 | tf_op jit(solution)/shard_map/all_gather | solution.py:209
  118.4 1.7 %shard_map.90 = (f32[32,172]{1,0:T(8,128)}, f32[32,256]{1,0:T(8,128)}) custom-call(s32[3]{0:T(128)} %copy-done.3, bf16[4,160,256]{2,1,0:T(8,128)(2,1)} %bitcast.9), custom_call_target="tpu_custom_call" | custom-call | tf_op jit(solution)/shard_map/pallas_call | solution.py:210
Async XLA Ops:
  0.6 78.9 %copy-start.7 = (s32[128]{0:T(128)S(1)}, s32[128]{0:T(128)}, u32[]{:S(2)}) copy-start(s32[128]{0:T(128)} %cols_ref.3) | copy-start | bytes 1540
  0.6 78.9 %copy-start.5 = (s32[128]{0:T(128)S(1)}, s32[128]{0:T(128)}, u32[]{:S(2)}) copy-start(s32[128]{0:T(128)} %rows_ref.3) | copy-start | bytes 1540
  39.0 28.5 %copy-start.3 = (s32[3]{0:T(128)}, s32[3]{0:T(128)S(1)}, u32[]{:S(2)}) copy-start(s32[3]{0:T(128)S(1)} %pad_add_fusion.where_ref) | copy-start | bytes 40
  39.0 2.2 %copy-start = (bf16[128,128,128]{2,1,0:T(8,128)(2,1)S(1)}, bf16[128,128,128]{2,1,0:T(8,128)(2,1)}, u32[]{:S(2)}) copy-start(bf16[128,128,128]{2,1,0:T(8,128)(2,1)} %tiles_ref.3) | copy-start | bytes 12582916
  41.2 0.7 copy-start.2
  41.9 0.7 copy-start.4
  42.6 0.7 copy-start.6
  43.2 0.7 copy-start.8
  79.5 2.2 %copy-start.1 = (bf16[128,128,128]{2,1,0:T(8,128)(2,1)S(1)}, bf16[128,128,128]{2,1,0:T(8,128)(2,1)}, u32[]{:S(2)}) copy-start(bf16[128,128,128]{2,1,0:T(8,128)(2,1)} %tiles_ref.3) | copy-start | bytes 12582916

commit v2 on v1

v2 whole, which is shorter than its diff:
```python
import jax
import jax.numpy as jnp
from jax import lax
from jax.experimental import pallas as pl
from jax.experimental.pallas import tpu as pltpu
from jax.sharding import Mesh
from jax.sharding import PartitionSpec as P

TILE = 128
STEP = 16
AXES = ("x", "zh", "zl", "y", "core")
ROW = ("x", "zh")
DEPTH = ("y", "core")
SMEM = pltpu.MemorySpace.SMEM
F32 = jnp.float32
BF16 = jnp.bfloat16
NT = (((1,), (1,)), ((), ()))
TN = (((0,), (0,)), ((), ()))


def prepare_kernel(weight_ref, labels_ref, out_ref):
    me = lax.axis_index("zl")
    weight = weight_ref[...].astype(F32)
    classes = weight.shape[1]
    mine = weight[0:8]
    for z in range(1, 4):
        mine = jnp.where(me == z, weight[8 * z : 8 * z + 8], mine)
    labels = labels_ref[...].astype(F32)
    rest = jnp.concatenate([mine[:, TILE:], jnp.zeros((8, 64 - (classes - TILE)), F32)], axis=1)
    for d in range(2):
        half = labels[:, d * TILE : d * TILE + TILE]
        both = jnp.concatenate([half[:, :64], half[:, 64:], jnp.zeros((6, 64), F32)], axis=0)
        right = jnp.concatenate([rest, both], axis=1)
        out_ref[d] = jnp.concatenate([mine[:, :TILE], right], axis=0).astype(BF16)


def fetch(pairs, sems):
    copies = [pltpu.make_async_copy(src, dst, sems.at[i]) for i, (src, dst) in enumerate(pairs)]
    for copy in copies:
        copy.start()
    return copies


def tile_copy(tiles_ref, held, sems, step):
    part = pl.ds(step * STEP, STEP)
    return pltpu.make_async_copy(tiles_ref.at[part], held.at[part], sems.at[step])


def forward_kernel(
    count_ref, rows_ref, cols_ref, source_ref, extra_ref, tiles_ref, out_ref,
    total, count, rows, cols, sems, held, tile_sems,
):
    steps = tiles_ref.shape[0] // STEP
    blocks = total.shape[0] - 1
    small = fetch([(count_ref, count), (rows_ref, rows), (cols_ref, cols)], sems)
    for step in range(steps):
        tile_copy(tiles_ref, held, tile_sems, step).start()
    total[...] = jnp.zeros_like(total)
    for copy in small:
        copy.wait()
    live = count[0]

    @pl.loop(0, steps)
    def work(step):
        tile_copy(tiles_ref, held, tile_sems, step).wait()
        products = []
        for j in range(STEP):
            col = cols[step * STEP + j]
            lanes = pl.ds(pl.multiple_of((col % 2) * TILE, TILE), TILE)
            products.append(
                lax.dot_general(
                    source_ref[col // 2, :, lanes], held[step * STEP + j], NT, preferred_element_type=F32
                )
            )
        for j in range(STEP):
            slot = step * STEP + j
            row = jnp.where(slot < live, rows[slot], blocks)
            total[row] = total[row] + products[j]

    for d in range(blocks):
        block = jnp.concatenate([total[d].astype(BF16), extra_ref[d % 2]], axis=0)
        for z in range(4):
            out_ref[z, d] = block


def middle_kernel(got_ref, out_ref, agg, weight_a, weight_b):
    me = lax.axis_index(DEPTH)
    for d in range(8):
        sums = got_ref[d, 0:32, :].astype(F32)
        for z in range(1, 4):
            sums = sums + got_ref[8 * z + d, 0:32, :].astype(F32)
        agg[32 * d : 32 * d + 32, :] = sums.astype(BF16)
        pieces = [got_ref[8 * z + d, 32:48, :].astype(F32) for z in range(4)]
        weight_a[32 * d : 32 * d + 32, :] = jnp.concatenate([p[0:8] for p in pieces], axis=0).astype(BF16)
        weight_b[32 * d : 32 * d + 32, :] = jnp.concatenate([p[8:16] for p in pieces], axis=0).astype(BF16)
    carrier = got_ref[(me // 2) * 8, 32:48, :].astype(F32)
    labels = jnp.concatenate([carrier[8:9, 64:], carrier[9:10, 64:]], axis=1)
    nodes = agg[...]
    wa = weight_a[...]
    wb = weight_b[...]
    ids = lax.broadcasted_iota(jnp.int32, (TILE, TILE), 0).astype(F32)
    exp_a = jnp.exp(lax.dot_general(wa, nodes, TN, preferred_element_type=F32))
    logit_b = lax.dot_general(wb, nodes, TN, preferred_element_type=F32)
    valid = ids < 172 - TILE
    exp_b = jnp.where(valid, jnp.exp(jnp.where(valid, logit_b, 0.0)), 0.0)
    whole = jnp.sum(exp_a, axis=0, keepdims=True) + jnp.sum(exp_b, axis=0, keepdims=True)
    delta_a = (exp_a / whole - jnp.where(ids == labels, 1.0, 0.0)).astype(BF16)
    delta_b = (exp_b / whole - jnp.where(ids + TILE == labels, 1.0, 0.0)).astype(BF16)
    hidden = jnp.dot(wa, delta_a, preferred_element_type=F32) + jnp.dot(wb, delta_b, preferred_element_type=F32)
    grad_a = lax.dot_general(nodes, delta_a, NT, preferred_element_type=F32)
    grad_b = lax.dot_general(nodes, delta_b, NT, preferred_element_type=F32)
    for d in range(8):
        out_ref[d, 0:32, :] = hidden[32 * d : 32 * d + 32].astype(BF16)
        out_ref[d, 32:64, :] = grad_a[32 * d : 32 * d + 32].astype(BF16)
        part = grad_b[32 * d : 32 * d + 32, :64]
        out_ref[d, 64:80, :] = jnp.concatenate([part[0:16], part[16:32]], axis=1).astype(BF16)


def backward_kernel(
    count_ref, rows_ref, cols_ref, got_ref, tiles_ref, out_ref,
    total, count, rows, cols, sems, held, tile_sems,
):
    steps = tiles_ref.shape[0] // STEP
    blocks = total.shape[0] - 1
    small = fetch([(count_ref, count), (rows_ref, rows), (cols_ref, cols)], sems)
    for step in range(steps):
        tile_copy(tiles_ref, held, tile_sems, step).start()
    total[...] = jnp.zeros_like(total)
    grad_a = got_ref[0, 32:64, :].astype(F32)
    grad_b = got_ref[0, 64:80, :].astype(F32)
    for d in range(1, 8):
        grad_a = grad_a + got_ref[d, 32:64, :].astype(F32)
        grad_b = grad_b + got_ref[d, 64:80, :].astype(F32)
    packed = jnp.concatenate(
        [
            jnp.concatenate([grad_a[0:16], grad_a[16:32]], axis=1),
            jnp.concatenate([grad_b[0:8], grad_b[8:16]], axis=1),
        ],
        axis=0,
    )
    for copy in small:
        copy.wait()
    live = count[0]

    @pl.loop(0, steps)
    def work(step):
        tile_copy(tiles_ref, held, tile_sems, step).wait()
        products = []
        for j in range(STEP):
            row = rows[step * STEP + j]
            products.append(
                jnp.dot(got_ref[row, 0:32, :], held[step * STEP + j], preferred_element_type=F32)
            )
        for j in range(STEP):
            slot = step * STEP + j
            col = jnp.where(slot < live, cols[slot], blocks)
            total[col] = total[col] + products[j]

    for peer in range(16):
        block = jnp.concatenate([total[2 * peer], total[2 * peer + 1]], axis=1)
        out_ref[peer] = jnp.concatenate([block, packed], axis=0).astype(BF16)


def final_kernel(got_ref, weight_ref, feature_ref):
    sums = got_ref[0].astype(F32)
    for peer in range(1, 16):
        sums = sums + got_ref[peer].astype(F32)
    feature_ref[...] = sums[0:32]
    grad_a = sums[32:48]
    grad_b = sums[48:56]
    weight_ref[0:16, 0:TILE] = grad_a[:, 0:TILE]
    weight_ref[16:32, 0:TILE] = grad_a[:, TILE:]
    for part in range(2):
        rows = grad_b[:, part * TILE : part * TILE + TILE]
        weight_ref[8 * part : 8 * part + 8, TILE:] = rows[:, 0:44]
        weight_ref[16 + 8 * part : 24 + 8 * part, TILE:] = rows[:, 64:108]


def body(features, weight, tile_values, tile_rows, tile_cols, tile_count, labels):
    shape = jax.ShapeDtypeStruct
    vmem = pl.BlockSpec(memory_space=pltpu.VMEM)
    far = pl.BlockSpec(memory_space=pltpu.MemorySpace.HBM)
    slots = tile_values.shape[0]
    scratch = [
        pltpu.SMEM((1,), jnp.int32),
        pltpu.SMEM((slots,), jnp.int32),
        pltpu.SMEM((slots,), jnp.int32),
        pltpu.SemaphoreType.DMA((3,)),
        pltpu.VMEM(tile_values.shape, BF16),
        pltpu.SemaphoreType.DMA((slots // STEP,)),
    ]
    params = pltpu.CompilerParams(vmem_limit_bytes=16 * 2**20)
    tile_params = pltpu.CompilerParams(vmem_limit_bytes=51 * 2**20)
    spread = jnp.broadcast_to(features[None], (16, *features.shape))
    source = lax.all_to_all(spread, ROW, 0, 0, tiled=True)
    extra = pl.pallas_call(
        prepare_kernel,
        in_specs=[vmem, vmem],
        out_specs=vmem,
        out_shape=shape((2, 16, TILE), BF16),
        compiler_params=params,
        cost_estimate=pl.CostEstimate(flops=10**10, bytes_accessed=0, transcendentals=0),
    )(weight, labels.reshape(1, -1))
    sent = pl.pallas_call(
        forward_kernel,
        in_specs=[far, far, far, vmem, vmem, far],
        out_specs=vmem,
        out_shape=shape((4, 8, 48, TILE), BF16),
        scratch_shapes=[pltpu.VMEM((9, 32, TILE), F32), *scratch],
        compiler_params=tile_params,
    )(tile_count, tile_rows, tile_cols, source, extra, tile_values)
    got = lax.all_to_all(sent.reshape(32, 48, TILE), ("zl", "y", "core"), 0, 0, tiled=True)
    back = pl.pallas_call(
        middle_kernel,
        in_specs=[vmem],
        out_specs=vmem,
        out_shape=shape((8, 80, TILE), BF16),
        scratch_shapes=[pltpu.VMEM((256, TILE), BF16)] * 3,
        compiler_params=params,
    )(got)
    grads = lax.all_to_all(back, DEPTH, 0, 0, tiled=True)
    parts = pl.pallas_call(
        backward_kernel,
        in_specs=[far, far, far, vmem, far],
        out_specs=vmem,
        out_shape=shape((16, 56, 256), BF16),
        scratch_shapes=[pltpu.VMEM((33, 32, TILE), F32), *scratch],
        compiler_params=tile_params,
    )(tile_count, tile_rows, tile_cols, grads, tile_values)
    ours = lax.all_to_all(parts, ROW, 0, 0, tiled=True)
    return pl.pallas_call(
        final_kernel,
        in_specs=[vmem],
        out_specs=(vmem, vmem),
        out_shape=(shape((32, 172), F32), shape((32, 256), F32)),
        compiler_params=params,
    )(ours)


def solution(mesh):
    fine = Mesh(mesh.devices.reshape(4, 4, 4, 4, 2), AXES)
    tiled = ("x", "zh", "zl")
    return jax.shard_map(
        body,
        mesh=fine,
        in_specs=(
            P(DEPTH, ("zl", "x", "zh")),
            P(DEPTH, None),
            P(tiled, None, None),
            P(tiled),
            P(tiled),
            P(tiled),
            P(tiled),
        ),
        out_specs=(P(DEPTH, None), P(DEPTH, ("zl", "x", "zh"))),
        check_vma=False,
    )
```

time: 121 us -> 113 us (0.934)
  the two profiles are of different devices: /device:TPU:32 before, /device:TPU:34 now
where the time goes in v2:
time: 113 us
  blocking collectives  63.7 us (56%)
  waiting for transfers between devices  18.6 us (16%)
  starting transfers between devices  17.2 us (15%)
  Pallas kernels  9.06 us (8%)
  local copies, waits for them, and re-layouts  2.84 us (3%)
  between operations  1.31 us (1%)
    all_to_all x1, blocking collectives, body(): ours = lax.all_to_all(parts, ROW, 0, 0, tiled=True)  35.1 us
    all_to_all x1, blocking collectives, body(): lax.all_to_all(sent.reshape(32, 48, TILE), ('zl', 'y', 'core'), 0, 0, til...  19.7 us
    all_to_all x1, waiting for transfers between devices, body(): source = lax.all_to_all(spread, ROW, 0, 0, tiled=True)  18.6 us
    all_to_all x1, starting transfers between devices, body(): source = lax.all_to_all(spread, ROW, 0, 0, tiled=True)  17.2 us
    all_to_all x1, blocking collectives, body(): grads = lax.all_to_all(back, DEPTH, 0, 0, tiled=True)  8.88 us
    pallas_call x1, Pallas kernels, body(): pl.pallas_call(forward_kernel, in_specs=[far, far, far, vmem, vmem, far],...  4.35 us
    pallas_call x1, Pallas kernels, body(): pl.pallas_call(backward_kernel, in_specs=[far, far, far, vmem, far], out_...  3.29 us
  transfers between devices with their start and end apart: 1, of which 1 were waited for; matrix products, arithmetic and copies ran while one was open for 0% of the time, Pallas kernels for 0%

profile of v2, /device:TPU:34, one launch (start us, length us, event | category | flops | bytes accessed | tf_op | source)
XLA Modules:
  0.0 112.7 jit_solution(10465979862321778069)
XLA Ops:
  0.6 1.4 %broadcast_in_dim.2 = bf16[16,32,256]{2,1,0:T(8,128)(2,1)} broadcast(bf16[32,256]{1,0:T(8,128)(2,1)} %param.7), dimensions={1,2} | broadcast | bytes 278528 | tf_op jit(solution)/shard_map/broadcast_in_dim | solution.py:194
  2.1 17.2 %all-to-all-start = ((bf16[16,32,256]{2,1,0:T(8,128)(2,1)}), bf16[16,32,256]{2,1,0:T(8,128)(2,1)S(1)}, u32[]{:S(2)}, u32[]{:S(2)}) async-start(bf16[16,32,256]{2,1,0:T(8,128)(2,1)} %broadcast_in_dim.2), calls=%async_computation | async-start | bytes 524288 | tf_op jit(solution)/shard_map/all_to_all | solution.py:195
  19.9 0.0 copy-start.2
  19.9 0.7 copy-done.2
  20.6 0.0 copy-start.3
  20.6 0.7 copy-done.3
  21.3 0.0 copy-start
  21.3 0.0 copy-start.1
  21.3 0.1 shard_map.86.extra_ref
  21.5 18.6 %all-to-all-done.source_ref = bf16[16,32,256]{2,1,0:T(8,128)(2,1)S(1)} async-done(((bf16[16,32,256]{2,1,0:T(8,128)(2,1)}), bf16[16,32,256]{2,1,0:T(8,128)(2,1)S(1)}, u32[]{:S(2)}, u32[]{:S(2)}) %all-to-all-start) | async-done | bytes 262176 | tf_op jit(solution)/shard_map/all_to_all | solution.py:195
  40.1 0.0 copy-done
  40.1 0.0 copy-done.1
  40.1 4.4 %shard_map.87 = bf16[4,8,48,128]{3,2,1,0:T(8,128)(2,1)S(1)} custom-call(s32[1]{0:T(128)S(6)} %copy.9.count_ref, s32[128]{0:T(128)S(1)} %copy-done, s32[128]{0:T(128)S(1)} %copy-done.1, bf16[16,32,256]{2,1,0:T(8,128)(2,1)S(1)} %all-to-all-done.source_ref, bf16[2,16,128]{2,1,0:T(8,128)(2,1)S(1)} %shard_map.86.extra_ref, bf16[128,128,128]{2,1,0:T(8,128)(2,1)} %tiles_ref.3), custom_call_target="tpu_custom_call" | custom-call | tf_op jit(solution)/shard_map/pallas_call | solution.py:204
  44.5 19.7 %all_to_all.20.got_ref = bf16[32,48,128]{2,1,0:T(8,128)(2,1)S(1)} all-to-all(bf16[32,48,128]{2,1,0:T(8,128)(2,1)S(1)} %bitcast.2), channel_id=1, replica_groups=mesh['x'=4,'zh'=4,'zl'=4,'y'=4,'core'=2] {'zl','y','core'}, dimensions={0} | all-to-all | bytes 786432 | tf_op jit(solution)/shard_map/all_to_all | solution.py:212
  64.2 0.6 shard_map.88
  64.8 8.9 %all_to_all.21.got_ref = bf16[8,80,128]{2,1,0:T(8,128)(2,1)S(1)} all-to-all(bf16[8,80,128]{2,1,0:T(8,128)(2,1)S(1)} %shard_map.88), channel_id=1, replica_groups=mesh['x'=4,'zh'=4,'zl'=4,'y'=4,'core'=2] {'y','core'}, dimensions={0} | all-to-all | bytes 327680 | tf_op jit(solution)/shard_map/all_to_all | solution.py:221
  73.6 3.3 %shard_map.89 = bf16[16,56,256]{2,1,0:T(8,128)(2,1)S(1)} custom-call(s32[1]{0:T(128)S(6)} %copy.9.count_ref, s32[128]{0:T(128)S(1)} %copy-done, s32[128]{0:T(128)S(1)} %copy-done.1, bf16[8,80,128]{2,1,0:T(8,128)(2,1)S(1)} %all_to_all.21.got_ref, bf16[128,128,128]{2,1,0:T(8,128)(2,1)} %tiles_ref.3), custom_call_target="tpu_custom_call" | custom-call | tf_op jit(solution)/shard_map/pallas_call | solution.py:222
  76.9 35.1 %all_to_all.22.got_ref = bf16[16,56,256]{2,1,0:T(8,128)(2,1)S(1)} all-to-all(bf16[16,56,256]{2,1,0:T(8,128)(2,1)S(1)} %shard_map.89), channel_id=1, replica_groups=mesh['x'=4,'zh'=4,'zl'=4,'y'=4,'core'=2] {'x','zh'}, dimensions={0} | all-to-all | bytes 917504 | tf_op jit(solution)/shard_map/all_to_all | solution.py:230
  112.0 0.7 shard_map.90
Async XLA Ops:
  2.1 38.0 %all-to-all-start = ((bf16[16,32,256]{2,1,0:T(8,128)(2,1)}), bf16[16,32,256]{2,1,0:T(8,128)(2,1)S(1)}, u32[]{:S(2)}, u32[]{:S(2)}) async-start(bf16[16,32,256]{2,1,0:T(8,128)(2,1)} %broadcast_in_dim.2), calls=%async_computation | async-start | bytes 524288 | tf_op jit(solution)/shard_map/all_to_all | solution.py:195
  19.9 0.7 copy-start.2
  20.6 0.7 copy-start.3
  21.3 18.8 %copy-start = (s32[128]{0:T(128)S(1)}, s32[128]{0:T(128)}, u32[]{:S(2)}) copy-start(s32[128]{0:T(128)} %rows_ref.3) | copy-start | bytes 1540
  21.3 18.8 %copy-start.1 = (s32[128]{0:T(128)S(1)}, s32[128]{0:T(128)}, u32[]{:S(2)}) copy-start(s32[128]{0:T(128)} %cols_ref.3) | copy-start | bytes 1540

commit v3 on v2

--- a/solution.py
+++ b/solution.py
@@ -9,7 +9,6 @@
 TILE = 128
 STEP = 16
 AXES = ("x", "zh", "zl", "y", "core")
-ROW = ("x", "zh")
 DEPTH = ("y", "core")
 SMEM = pltpu.MemorySpace.SMEM
 F32 = jnp.float32
@@ -156,14 +155,22 @@
             col = jnp.where(slot < live, cols[slot], blocks)
             total[col] = total[col] + products[j]
 
-    for peer in range(16):
-        block = jnp.concatenate([total[2 * peer], total[2 * peer + 1]], axis=1)
-        out_ref[peer] = jnp.concatenate([block, packed], axis=0).astype(BF16)
+    for x in range(4):
+        blocks_of = [jnp.concatenate([total[2 * p], total[2 * p + 1]], axis=1) for p in range(4 * x, 4 * x + 4)]
+        out_ref[x] = jnp.concatenate([*blocks_of, packed], axis=0).astype(BF16)
+
+
+def sum_kernel(got_ref, out_ref):
+    sums = got_ref[0].astype(F32)
+    for x in range(1, 4):
+        sums = sums + got_ref[x].astype(F32)
+    for z in range(4):
+        out_ref[z] = jnp.concatenate([sums[32 * z : 32 * z + 32], sums[128:152]], axis=0).astype(BF16)
 
 
 def final_kernel(got_ref, weight_ref, feature_ref):
     sums = got_ref[0].astype(F32)
-    for peer in range(1, 16):
+    for peer in range(1, 4):
         sums = sums + got_ref[peer].astype(F32)
     feature_ref[...] = sums[0:32]
     grad_a = sums[32:48]
@@ -191,8 +198,9 @@
     ]
     params = pltpu.CompilerParams(vmem_limit_bytes=16 * 2**20)
     tile_params = pltpu.CompilerParams(vmem_limit_bytes=51 * 2**20)
-    spread = jnp.broadcast_to(features[None], (16, *features.shape))
-    source = lax.all_to_all(spread, ROW, 0, 0, tiled=True)
+    near = lax.all_gather(features, "zh", axis=0)
+    spread = jnp.broadcast_to(near[None], (4, *near.shape))
+    source = lax.all_to_all(spread, "x", 0, 0, tiled=True).reshape(16, *features.shape)
     extra = pl.pallas_call(
         prepare_kernel,
         in_specs=[vmem, vmem],
@@ -223,11 +231,19 @@
         backward_kernel,
         in_specs=[far, far, far, vmem, far],
         out_specs=vmem,
-        out_shape=shape((16, 56, 256), BF16),
+        out_shape=shape((4, 152, 256), BF16),
         scratch_shapes=[pltpu.VMEM((33, 32, TILE), F32), *scratch],
         compiler_params=tile_params,
     )(tile_count, tile_rows, tile_cols, grads, tile_values)
-    ours = lax.all_to_all(parts, ROW, 0, 0, tiled=True)
+    lines = lax.all_to_all(parts, "x", 0, 0, tiled=True)
+    summed = pl.pallas_call(
+        sum_kernel,
+        in_specs=[vmem],
+        out_specs=vmem,
+        out_shape=shape((4, 56, 256), BF16),
+        compiler_params=params,
+    )(lines)
+    ours = lax.all_to_all(summed, "zh", 0, 0, tiled=True)
     return pl.pallas_call(
         final_kernel,
         in_specs=[vmem],

time: 113 us -> 105 us (0.929)
  the two profiles are of different devices: /device:TPU:34 before, /device:TPU:32 now
where the time goes in v3:
time: 105 us
  blocking collectives  83.9 us (80%)
  Pallas kernels  9.01 us (9%)
  waiting for transfers between devices  4.48 us (4%)
  starting transfers between devices  4.29 us (4%)
  local copies, waits for them, and re-layouts  2.13 us (2%)
  between operations  1.31 us (1%)
    all_gather x1, blocking collectives, body(): near = lax.all_gather(features, 'zh', axis=0)  25 us
    all_to_all x1, blocking collectives, body(): ours = lax.all_to_all(summed, 'zh', 0, 0, tiled=True)  20.8 us
    all_to_all x1, blocking collectives, body(): lax.all_to_all(sent.reshape(32, 48, TILE), ('zl', 'y', 'core'), 0, 0, til...  19.6 us
    all_to_all x1, blocking collectives, body(): lines = lax.all_to_all(parts, 'x', 0, 0, tiled=True)  9.61 us
    all_to_all x1, blocking collectives, body(): grads = lax.all_to_all(back, DEPTH, 0, 0, tiled=True)  8.88 us
    all_to_all x1, waiting for transfers between devices, body(): lax.all_to_all(spread, 'x', 0, 0, tiled=True).reshape(16, *features.shape)  4.48 us
    pallas_call x1, Pallas kernels, body(): pl.pallas_call(forward_kernel, in_specs=[far, far, far, vmem, vmem, far],...  4.31 us
    all_to_all x1, starting transfers between devices, body(): lax.all_to_all(spread, 'x', 0, 0, tiled=True).reshape(16, *features.shape)  4.29 us
  transfers between devices with their start and end apart: 1, of which 1 were waited for; matrix products, arithmetic and copies ran while one was open for 0% of the time, Pallas kernels for 0%

profile of v3, /device:TPU:32, one launch (start us, length us, event | category | flops | bytes accessed | tf_op | source)
XLA Modules:
  0.0 105.1 jit_solution(18312471487963285278)
XLA Ops:
  0.6 25.0 %all-gather = bf16[128,256]{1,0:T(8,128)(2,1)S(1)} all-gather(bf16[32,256]{1,0:T(8,128)(2,1)} %param.7), channel_id=2, replica_groups=mesh['x'=4,'zh'=4,'zl'=4,'y'=4,'core'=2] {'zh'}, dimensions={0}, use_global_device_ids=true | all-gather | bytes 81920 | tf_op jit(solution)/shard_map/all_gather | solution.py:201
  25.6 0.7 broadcast_in_dim.2
  26.4 4.3 %all-to-all-start = ((bf16[4,4,32,256]{3,2,1,0:T(8,128)(2,1)}), bf16[4,4,32,256]{3,2,1,0:T(8,128)(2,1)S(1)}, u32[]{:S(2)}, u32[]{:S(2)}) async-start(bf16[4,4,32,256]{3,2,1,0:T(8,128)(2,1)} %broadcast_in_dim.2), calls=%async_computation | async-start | bytes 524288 | tf_op jit(solution)/shard_map/all_to_all | solution.py:203
  30.7 0.0 copy-start.2
  30.7 0.7 copy-done.2
  31.4 0.0 copy-start.3
  31.4 0.7 copy-done.3
  32.1 0.0 copy-start
  32.1 0.0 copy-start.1
  32.1 0.1 shard_map.86.extra_ref
  32.9 4.5 %all-to-all-done = bf16[4,4,32,256]{3,2,1,0:T(8,128)(2,1)S(1)} async-done(((bf16[4,4,32,256]{3,2,1,0:T(8,128)(2,1)}), bf16[4,4,32,256]{3,2,1,0:T(8,128)(2,1)S(1)}, u32[]{:S(2)}, u32[]{:S(2)}) %all-to-all-start) | async-done | bytes 262176 | tf_op jit(solution)/shard_map/all_to_all | solution.py:203
  37.3 0.0 copy-done
  37.3 0.0 copy-done.1
  37.3 4.3 %shard_map.87 = bf16[4,8,48,128]{3,2,1,0:T(8,128)(2,1)S(1)} custom-call(s32[1]{0:T(128)S(6)} %copy.9.count_ref, s32[128]{0:T(128)S(1)} %copy-done, s32[128]{0:T(128)S(1)} %copy-done.1, bf16[16,32,256]{2,1,0:T(8,128)(2,1)S(1)} %bitcast.5, bf16[2,16,128]{2,1,0:T(8,128)(2,1)S(1)} %shard_map.86.extra_ref, bf16[128,128,128]{2,1,0:T(8,128)(2,1)} %tiles_ref.3), custom_call_target="tpu_custom_call" | custom-call | tf_op jit(solution)/shard_map/pallas_call | solution.py:212
  41.7 19.6 %all_to_all.25.got_ref = bf16[32,48,128]{2,1,0:T(8,128)(2,1)S(1)} all-to-all(bf16[32,48,128]{2,1,0:T(8,128)(2,1)S(1)} %bitcast.4), channel_id=1, replica_groups=mesh['x'=4,'zh'=4,'zl'=4,'y'=4,'core'=2] {'zl','y','core'}, dimensions={0} | all-to-all | bytes 786432 | tf_op jit(solution)/shard_map/all_to_all | solution.py:220
  61.2 0.6 shard_map.88
  61.8 8.9 %all_to_all.26.got_ref = bf16[8,80,128]{2,1,0:T(8,128)(2,1)S(1)} all-to-all(bf16[8,80,128]{2,1,0:T(8,128)(2,1)S(1)} %shard_map.88), channel_id=1, replica_groups=mesh['x'=4,'zh'=4,'zl'=4,'y'=4,'core'=2] {'y','core'}, dimensions={0} | all-to-all | bytes 327680 | tf_op jit(solution)/shard_map/all_to_all | solution.py:229
  70.7 3.3 %shard_map.89 = bf16[4,152,256]{2,1,0:T(8,128)(2,1)S(1)} custom-call(s32[1]{0:T(128)S(6)} %copy.9.count_ref, s32[128]{0:T(128)S(1)} %copy-done, s32[128]{0:T(128)S(1)} %copy-done.1, bf16[8,80,128]{2,1,0:T(8,128)(2,1)S(1)} %all_to_all.26.got_ref, bf16[128,128,128]{2,1,0:T(8,128)(2,1)} %tiles_ref.3), custom_call_target="tpu_custom_call" | custom-call | tf_op jit(solution)/shard_map/pallas_call | solution.py:230
  73.9 9.6 %all_to_all.27.got_ref = bf16[4,152,256]{2,1,0:T(8,128)(2,1)S(1)} all-to-all(bf16[4,152,256]{2,1,0:T(8,128)(2,1)S(1)} %shard_map.89), channel_id=1, replica_groups=mesh['x'=4,'zh'=4,'zl'=4,'y'=4,'core'=2] {'x'}, dimensions={0} | all-to-all | bytes 622592 | tf_op jit(solution)/shard_map/all_to_all | solution.py:238
  83.6 20.8 %all_to_all.28.got_ref = bf16[4,56,256]{2,1,0:T(8,128)(2,1)S(1)} all-to-all(bf16[4,56,256]{2,1,0:T(8,128)(2,1)S(1)} %shard_map.90), channel_id=1, replica_groups=mesh['x'=4,'zh'=4,'zl'=4,'y'=4,'core'=2] {'zh'}, dimensions={0} | all-to-all | bytes 229376 | tf_op jit(solution)/shard_map/all_to_all | solution.py:246
  104.4 0.7 shard_map.91
  (1 shorter events, 0.0 us)
Async XLA Ops:
  26.4 11.0 %all-to-all-start = ((bf16[4,4,32,256]{3,2,1,0:T(8,128)(2,1)}), bf16[4,4,32,256]{3,2,1,0:T(8,128)(2,1)S(1)}, u32[]{:S(2)}, u32[]{:S(2)}) async-start(bf16[4,4,32,256]{3,2,1,0:T(8,128)(2,1)} %broadcast_in_dim.2), calls=%async_computation | async-start | bytes 524288 | tf_op jit(solution)/shard_map/all_to_all | solution.py:203
  30.7 0.7 copy-start.2
  31.4 0.7 copy-start.3
  32.1 5.3 %copy-start = (s32[128]{0:T(128)S(1)}, s32[128]{0:T(128)}, u32[]{:S(2)}) copy-start(s32[128]{0:T(128)} %rows_ref.3) | copy-start | bytes 1540
  32.1 5.3 %copy-start.1 = (s32[128]{0:T(128)S(1)}, s32[128]{0:T(128)}, u32[]{:S(2)}) copy-start(s32[128]{0:T(128)} %cols_ref.3) | copy-start | bytes 1540

commit v4 on v3

--- a/solution.py
+++ b/solution.py
@@ -7,7 +7,7 @@
 from jax.sharding import PartitionSpec as P
 
 TILE = 128
-STEP = 16
+STEP = 32
 AXES = ("x", "zh", "zl", "y", "core")
 DEPTH = ("y", "core")
 SMEM = pltpu.MemorySpace.SMEM
@@ -17,20 +17,15 @@
 TN = (((0,), (0,)), ((), ()))
 
 
-def prepare_kernel(weight_ref, labels_ref, out_ref):
-    me = lax.axis_index("zl")
+def prepare_kernel(near_ref, weight_ref, spread_ref, out_ref):
+    for x in range(4):
+        spread_ref[x] = near_ref[...]
     weight = weight_ref[...].astype(F32)
-    classes = weight.shape[1]
-    mine = weight[0:8]
-    for z in range(1, 4):
-        mine = jnp.where(me == z, weight[8 * z : 8 * z + 8], mine)
-    labels = labels_ref[...].astype(F32)
-    rest = jnp.concatenate([mine[:, TILE:], jnp.zeros((8, 64 - (classes - TILE)), F32)], axis=1)
-    for d in range(2):
-        half = labels[:, d * TILE : d * TILE + TILE]
-        both = jnp.concatenate([half[:, :64], half[:, 64:], jnp.zeros((6, 64), F32)], axis=0)
-        right = jnp.concatenate([rest, both], axis=1)
-        out_ref[d] = jnp.concatenate([mine[:, :TILE], right], axis=0).astype(BF16)
+    hidden, classes = weight.shape
+    rest = jnp.concatenate([weight[:, TILE:], jnp.zeros((hidden, 2 * TILE - classes), F32)], axis=1)
+    out_ref[...] = jnp.zeros_like(out_ref)
+    out_ref[0:hidden, :] = weight[:, :TILE].astype(BF16)
+    out_ref[hidden : 2 * hidden, :] = rest.astype(BF16)
 
 
 def fetch(pairs, sems):
@@ -46,10 +41,9 @@
 
 
 def forward_kernel(
-    count_ref, rows_ref, cols_ref, source_ref, extra_ref, tiles_ref, out_ref,
-    total, count, rows, cols, sems, held, tile_sems,
+    count_ref, rows_ref, cols_ref, source_ref, tiles_ref, out_ref, total, count, rows, cols, sems, held, tile_sems
 ):
-    steps = tiles_ref.shape[0] // STEP
+    steps = held.shape[0] // STEP
     blocks = total.shape[0] - 1
     small = fetch([(count_ref, count), (rows_ref, rows), (cols_ref, cols)], sems)
     for step in range(steps):
@@ -76,50 +70,54 @@
             row = jnp.where(slot < live, rows[slot], blocks)
             total[row] = total[row] + products[j]
 
-    for d in range(blocks):
-        block = jnp.concatenate([total[d].astype(BF16), extra_ref[d % 2]], axis=0)
-        for z in range(4):
-            out_ref[z, d] = block
-
-
-def middle_kernel(got_ref, out_ref, agg, weight_a, weight_b):
-    me = lax.axis_index(DEPTH)
+    for p in range(blocks):
+        block = total[p].astype(BF16)
+        for y in range(4):
+            out_ref[p // 2, y, p % 2] = block
+
+
+def middle_kernel(got_ref, wide_ref, labels_ref, out_ref, agg, weight_a, weight_b, held, sem):
+    copy = pltpu.make_async_copy(wide_ref.at[:, 0:64, :], held, sem)
+    copy.start()
+    y = lax.axis_index("y")
+    core = lax.axis_index("core")
     for d in range(8):
-        sums = got_ref[d, 0:32, :].astype(F32)
+        sums = got_ref[d].astype(F32)
         for z in range(1, 4):
-            sums = sums + got_ref[8 * z + d, 0:32, :].astype(F32)
+            sums = sums + got_ref[8 * z + d].astype(F32)
         agg[32 * d : 32 * d + 32, :] = sums.astype(BF16)
-        pieces = [got_ref[8 * z + d, 32:48, :].astype(F32) for z in range(4)]
-        weight_a[32 * d : 32 * d + 32, :] = jnp.concatenate([p[0:8] for p in pieces], axis=0).astype(BF16)
-        weight_b[32 * d : 32 * d + 32, :] = jnp.concatenate([p[8:16] for p in pieces], axis=0).astype(BF16)
-    carrier = got_ref[(me // 2) * 8, 32:48, :].astype(F32)
-    labels = jnp.concatenate([carrier[8:9, 64:], carrier[9:10, 64:]], axis=1)
+    copy.wait()
+    for d in range(8):
+        weight_a[32 * d : 32 * d + 32, :] = held[d, 0:32, :]
+        weight_b[32 * d : 32 * d + 32, :] = held[d, 32:64, :]
+    both = labels_ref[...]
+    labels = jnp.where(core == 0, both[:, :TILE], both[:, TILE:])
     nodes = agg[...]
-    wa = weight_a[...]
-    wb = weight_b[...]
-    ids = lax.broadcasted_iota(jnp.int32, (TILE, TILE), 0).astype(F32)
-    exp_a = jnp.exp(lax.dot_general(wa, nodes, TN, preferred_element_type=F32))
-    logit_b = lax.dot_general(wb, nodes, TN, preferred_element_type=F32)
-    valid = ids < 172 - TILE
-    exp_b = jnp.where(valid, jnp.exp(jnp.where(valid, logit_b, 0.0)), 0.0)
+    ids = lax.broadcasted_iota(jnp.int32, (TILE, TILE), 0)
+    exp_a = jnp.exp(lax.dot_general(weight_a[...], nodes, TN, preferred_element_type=F32))
+    logit_b = lax.dot_general(weight_b[...], nodes, TN, preferred_element_type=F32)
+    exp_b = jnp.where(ids < 172 - TILE, jnp.exp(logit_b), 0.0)
     whole = jnp.sum(exp_a, axis=0, keepdims=True) + jnp.sum(exp_b, axis=0, keepdims=True)
     delta_a = (exp_a / whole - jnp.where(ids == labels, 1.0, 0.0)).astype(BF16)
     delta_b = (exp_b / whole - jnp.where(ids + TILE == labels, 1.0, 0.0)).astype(BF16)
-    hidden = jnp.dot(wa, delta_a, preferred_element_type=F32) + jnp.dot(wb, delta_b, preferred_element_type=F32)
-    grad_a = lax.dot_general(nodes, delta_a, NT, preferred_element_type=F32)
-    grad_b = lax.dot_general(nodes, delta_b, NT, preferred_element_type=F32)
-    for d in range(8):
-        out_ref[d, 0:32, :] = hidden[32 * d : 32 * d + 32].astype(BF16)
-        out_ref[d, 32:64, :] = grad_a[32 * d : 32 * d + 32].astype(BF16)
-        part = grad_b[32 * d : 32 * d + 32, :64]
-        out_ref[d, 64:80, :] = jnp.concatenate([part[0:16], part[16:32]], axis=1).astype(BF16)
+    mine = pl.ds(pl.multiple_of(y * 64, 64), 64)
+    hidden = jnp.dot(weight_a[mine, :], delta_a, preferred_element_type=F32)
+    hidden = hidden + jnp.dot(weight_b[mine, :], delta_b, preferred_element_type=F32)
+    grad_a = lax.dot_general(agg[mine, :], delta_a, NT, preferred_element_type=F32)
+    grad_b = lax.dot_general(agg[mine, :], delta_b, NT, preferred_element_type=F32)
+    for c in range(2):
+        part = grad_b[32 * c : 32 * c + 32, :64]
+        packed = jnp.concatenate([part[0:16], part[16:32]], axis=1)
+        block = jnp.concatenate([hidden[32 * c : 32 * c + 32], grad_a[32 * c : 32 * c + 32], packed], axis=0)
+        for z in range(4):
+            out_ref[2 * z + c] = block.astype(BF16)
 
 
 def backward_kernel(
     count_ref, rows_ref, cols_ref, got_ref, tiles_ref, out_ref,
     total, count, rows, cols, sems, held, tile_sems,
 ):
-    steps = tiles_ref.shape[0] // STEP
+    steps = held.shape[0] // STEP
     blocks = total.shape[0] - 1
     small = fetch([(count_ref, count), (rows_ref, rows), (cols_ref, cols)], sems)
     for step in range(steps):
@@ -196,37 +194,39 @@
         pltpu.VMEM(tile_values.shape, BF16),
         pltpu.SemaphoreType.DMA((slots // STEP,)),
     ]
+    middle_params = pltpu.CompilerParams(vmem_limit_bytes=213 * 2**18)
+    tile_params = pltpu.CompilerParams(vmem_limit_bytes=51 * 2**20)
     params = pltpu.CompilerParams(vmem_limit_bytes=16 * 2**20)
-    tile_params = pltpu.CompilerParams(vmem_limit_bytes=51 * 2**20)
     near = lax.all_gather(features, "zh", axis=0)
-    spread = jnp.broadcast_to(near[None], (4, *near.shape))
-    source = lax.all_to_all(spread, "x", 0, 0, tiled=True).reshape(16, *features.shape)
-    extra = pl.pallas_call(
+    spread, padded = pl.pallas_call(
         prepare_kernel,
         in_specs=[vmem, vmem],
-        out_specs=vmem,
-        out_shape=shape((2, 16, TILE), BF16),
+        out_specs=(vmem, vmem),
+        out_shape=(shape((4, *near.shape), BF16), shape((512, TILE), BF16)),
         compiler_params=params,
         cost_estimate=pl.CostEstimate(flops=10**10, bytes_accessed=0, transcendentals=0),
-    )(weight, labels.reshape(1, -1))
+    )(near, weight)
+    wide = lax.all_gather(padded, DEPTH, axis=0)
+    source = lax.all_to_all(spread, "x", 0, 0, tiled=True).reshape(16, *features.shape)
     sent = pl.pallas_call(
         forward_kernel,
-        in_specs=[far, far, far, vmem, vmem, far],
-        out_specs=vmem,
-        out_shape=shape((4, 8, 48, TILE), BF16),
+        in_specs=[far, far, far, vmem, far],
+        out_specs=vmem,
+        out_shape=shape((4, 4, 2, 32, TILE), BF16),
         scratch_shapes=[pltpu.VMEM((9, 32, TILE), F32), *scratch],
         compiler_params=tile_params,
-    )(tile_count, tile_rows, tile_cols, source, extra, tile_values)
-    got = lax.all_to_all(sent.reshape(32, 48, TILE), ("zl", "y", "core"), 0, 0, tiled=True)
+    )(tile_count, tile_rows, tile_cols, source, tile_values)
+    got = lax.all_to_all(sent.reshape(32, 32, TILE), ("zl", "y", "core"), 0, 0, tiled=True)
     back = pl.pallas_call(
         middle_kernel,
-        in_specs=[vmem],
+        in_specs=[vmem, far, vmem],
         out_specs=vmem,
         out_shape=shape((8, 80, TILE), BF16),
-        scratch_shapes=[pltpu.VMEM((256, TILE), BF16)] * 3,
-        compiler_params=params,
-    )(got)
-    grads = lax.all_to_all(back, DEPTH, 0, 0, tiled=True)
+        scratch_shapes=[pltpu.VMEM((256, TILE), BF16)] * 3
+        + [pltpu.VMEM((8, 64, TILE), BF16), pltpu.SemaphoreType.DMA],
+        compiler_params=middle_params,
+    )(got, wide, labels.reshape(1, -1))
+    grads = lax.all_to_all(back, ("zl", "core"), 0, 0, tiled=True)
     parts = pl.pallas_call(
         backward_kernel,
         in_specs=[far, far, far, vmem, far],

time: 105 us -> 121 us (1.15)
  the two profiles are of different devices: /device:TPU:32 before, /device:TPU:2 now
where the time goes in v4:
time: 121 us; the launch traced here: 120 us
  blocking collectives  85.3 us (70%)
  between operations  14.7 us (12%)
  Pallas kernels  9.95 us (8%)
  starting transfers between devices  4.87 us (4%)
  waiting for transfers between devices  4.59 us (4%)
    all_gather x1, blocking collectives, body(): near = lax.all_gather(features, 'zh', axis=0)  25.9 us
    all_to_all x1, blocking collectives, body(): ours = lax.all_to_all(summed, 'zh', 0, 0, tiled=True)  22.4 us
    all_to_all x1, blocking collectives, body(): lax.all_to_all(sent.reshape(32, 32, TILE), ('zl', 'y', 'core'), 0, 0, til...  17.1 us
    all_to_all x1, blocking collectives, body(): lines = lax.all_to_all(parts, 'x', 0, 0, tiled=True)  10.2 us
    all_to_all x1, blocking collectives, body(): grads = lax.all_to_all(back, ('zl', 'core'), 0, 0, tiled=True)  9.71 us
    all_to_all x1, starting transfers between devices, body(): lax.all_to_all(spread, 'x', 0, 0, tiled=True).reshape(16, *features.shape)  4.84 us
    all_to_all x1, waiting for transfers between devices, body(): lax.all_to_all(spread, 'x', 0, 0, tiled=True).reshape(16, *features.shape)  4.57 us
    pallas_call x1, Pallas kernels, body(): pl.pallas_call(forward_kernel, in_specs=[far, far, far, vmem, far], out_s...  4.01 us
  transfers between devices with their start and end apart: 2, of which 1 were waited for; matrix products, arithmetic and copies ran while one was open for 0% of the time, Pallas kernels for 3%

profile of v4, /device:TPU:2, one launch (start us, length us, event | category | flops | bytes accessed | tf_op | source)
XLA Modules:
  0.0 120.2 jit_solution(16620569106185078994)
XLA Ops:
  7.2 0.0 all-gather.4.cloned.1.call-start
  7.2 25.9 %all-gather = bf16[128,256]{1,0:T(8,128)(2,1)S(1)} all-gather(bf16[32,256]{1,0:T(8,128)(2,1)} %param.7), channel_id=2, replica_groups=mesh['x'=4,'zh'=4,'zl'=4,'y'=4,'core'=2] {'zh'}, dimensions={0}, use_global_device_ids=true | all-gather | bytes 81920 | tf_op jit(solution)/shard_map/all_gather | solution.py:200
  33.1 0.0 copy-start.3
  33.1 0.7 copy-done.3
  33.8 0.0 copy-start
  33.8 0.0 copy-start.1
  33.8 0.8 shard_map.86
  34.6 0.0 copy-start.2
  34.6 0.0 all-gather.4.cloned.1.call-update
  34.7 4.8 %all-to-all-start = ((bf16[4,4,32,256]{3,2,1,0:T(8,128)(2,1)}), bf16[4,4,32,256]{3,2,1,0:T(8,128)(2,1)S(1)}, u32[]{:S(2)}, u32[]{:S(2)}) async-start(bf16[4,4,32,256]{3,2,1,0:T(8,128)(2,1)} %get-tuple-element.4), calls=%async_computation | async-start | bytes 524288 | tf_op jit(solution)/shard_map/all_to_all | solution.py:210
  40.2 4.6 %all-to-all-done = bf16[4,4,32,256]{3,2,1,0:T(8,128)(2,1)S(1)} async-done(((bf16[4,4,32,256]{3,2,1,0:T(8,128)(2,1)}), bf16[4,4,32,256]{3,2,1,0:T(8,128)(2,1)S(1)}, u32[]{:S(2)}, u32[]{:S(2)}) %all-to-all-start) | async-done | bytes 262176 | tf_op jit(solution)/shard_map/all_to_all | solution.py:210
  44.7 0.0 copy-done
  44.7 0.0 copy-done.1
  44.7 4.0 %shard_map.87 = bf16[4,4,2,32,128]{4,3,2,1,0:T(8,128)(2,1)S(1)} custom-call(s32[1]{0:T(128)S(6)} %copy.9.count_ref, s32[128]{0:T(128)S(1)} %copy-done, s32[128]{0:T(128)S(1)} %copy-done.1, bf16[16,32,256]{2,1,0:T(8,128)(2,1)S(1)} %bitcast.5, bf16[128,128,128]{2,1,0:T(8,128)(2,1)} %tiles_ref.3), custom_call_target="tpu_custom_call" | custom-call | tf_op jit(solution)/shard_map/pallas_call | solution.py:211
  48.8 17.1 %all_to_all.25.got_ref = bf16[32,32,128]{2,1,0:T(8,128)(2,1)S(1)} all-to-all(bf16[32,32,128]{2,1,0:T(8,128)(2,1)S(1)} %bitcast.6), channel_id=1, replica_groups=mesh['x'=4,'zh'=4,'zl'=4,'y'=4,'core'=2] {'zl','y','core'}, dimensions={0} | all-to-all | bytes 524288 | tf_op jit(solution)/shard_map/all_to_all | solution.py:219
  65.9 0.0 all-gather.4.cloned.1.call-done
  65.9 0.0 copy-done.2
  65.9 1.4 %shard_map.88 = bf16[8,80,128]{2,1,0:T(8,128)(2,1)S(1)} custom-call(bf16[32,32,128]{2,1,0:T(8,128)(2,1)S(1)} %all_to_all.25.got_ref, bf16[8,512,128]{2,1,0:T(8,128)(2,1)} %bitcast.9, s32[1,256]{1,0:T(1,128)S(1)} %bitcast.8), custom_call_target="tpu_custom_call" | custom-call | tf_op jit(solution)/shard_map/pallas_call | solution.py:220
  67.3 9.7 %all_to_all.26.got_ref = bf16[8,80,128]{2,1,0:T(8,128)(2,1)S(1)} all-to-all(bf16[8,80,128]{2,1,0:T(8,128)(2,1)S(1)} %shard_map.88), channel_id=1, replica_groups=mesh['x'=4,'zh'=4,'zl'=4,'y'=4,'core'=2] {'zl','core'}, dimensions={0} | all-to-all | bytes 327680 | tf_op jit(solution)/shard_map/all_to_all | solution.py:229
  77.0 3.0 %shard_map.89 = bf16[4,152,256]{2,1,0:T(8,128)(2,1)S(1)} custom-call(s32[1]{0:T(128)S(6)} %copy.9.count_ref, s32[128]{0:T(128)S(1)} %copy-done, s32[128]{0:T(128)S(1)} %copy-done.1, bf16[8,80,128]{2,1,0:T(8,128)(2,1)S(1)} %all_to_all.26.got_ref, bf16[128,128,128]{2,1,0:T(8,128)(2,1)} %tiles_ref.3), custom_call_target="tpu_custom_call" | custom-call | tf_op jit(solution)/shard_map/pallas_call | solution.py:230
  80.0 10.2 %all_to_all.27.got_ref = bf16[4,152,256]{2,1,0:T(8,128)(2,1)S(1)} all-to-all(bf16[4,152,256]{2,1,0:T(8,128)(2,1)S(1)} %shard_map.89), channel_id=1, replica_groups=mesh['x'=4,'zh'=4,'zl'=4,'y'=4,'core'=2] {'x'}, dimensions={0} | all-to-all | bytes 622592 | tf_op jit(solution)/shard_map/all_to_all | solution.py:238
  90.2 22.4 %all_to_all.28.got_ref = bf16[4,56,256]{2,1,0:T(8,128)(2,1)S(1)} all-to-all(bf16[4,56,256]{2,1,0:T(8,128)(2,1)S(1)} %shard_map.90), channel_id=1, replica_groups=mesh['x'=4,'zh'=4,'zl'=4,'y'=4,'core'=2] {'zh'}, dimensions={0} | all-to-all | bytes 229376 | tf_op jit(solution)/shard_map/all_to_all | solution.py:246
  112.6 0.7 shard_map.91
  (1 shorter events, 0.0 us)
Async XLA Ops:
  7.2 58.7 %all-gather.4.cloned.1.call-start = ((), (), s32[]{:S(2)}) async-start(), calls=%async_computation.5 | async-start | bytes 1179648 | tf_op jit(solution)/shard_map/all_gather | solution.py:209
  33.1 0.7 copy-start.3
  33.8 10.9 %copy-start = (s32[128]{0:T(128)S(1)}, s32[128]{0:T(128)}, u32[]{:S(2)}) copy-start(s32[128]{0:T(128)} %rows_ref.3) | copy-start | bytes 1540
  33.8 10.9 %copy-start.1 = (s32[128]{0:T(128)S(1)}, s32[128]{0:T(128)}, u32[]{:S(2)}) copy-start(s32[128]{0:T(128)} %cols_ref.3) | copy-start | bytes 1540
  34.6 31.2 %copy-start.2 = (s32[256]{0:T(256)S(1)}, s32[256]{0:T(256)}, u32[]{:S(2)}) copy-start(s32[256]{0:T(256)} %param.13) | copy-start | bytes 3076
  34.7 10.1 %all-to-all-start = ((bf16[4,4,32,256]{3,2,1,0:T(8,128)(2,1)}), bf16[4,4,32,256]{3,2,1,0:T(8,128)(2,1)S(1)}, u32[]{:S(2)}, u32[]{:S(2)}) async-start(bf16[4,4,32,256]{3,2,1,0:T(8,128)(2,1)} %get-tuple-element.4), calls=%async_computation | async-start | bytes 524288 | tf_op jit(solution)/shard_map/all_to_all | solution.py:210
Sparse Core Ops, SparseCore 0:
  34.8 27.5 all-gather.3

commit v5 on v3

--- a/solution.py
+++ b/solution.py
@@ -7,17 +7,21 @@
 from jax.sharding import PartitionSpec as P
 
 TILE = 128
-STEP = 16
+STEP = 64
 AXES = ("x", "zh", "zl", "y", "core")
 DEPTH = ("y", "core")
-SMEM = pltpu.MemorySpace.SMEM
 F32 = jnp.float32
 BF16 = jnp.bfloat16
 NT = (((1,), (1,)), ((), ()))
 TN = (((0,), (0,)), ((), ()))
 
 
-def prepare_kernel(weight_ref, labels_ref, out_ref):
+def prepare_kernel(
+    count_ref, weight_ref, labels_ref, rows_ref, cols_ref, out_ref, row_to_ref, col_to_ref
+):
+    live = lax.broadcasted_iota(jnp.int32, rows_ref.shape, 1) < count_ref[0]
+    row_to_ref[...] = jnp.where(live, rows_ref[...], 8)
+    col_to_ref[...] = jnp.where(live, cols_ref[...], 32)
     me = lax.axis_index("zl")
     weight = weight_ref[...].astype(F32)
     classes = weight.shape[1]
@@ -33,47 +37,39 @@
         out_ref[d] = jnp.concatenate([mine[:, :TILE], right], axis=0).astype(BF16)
 
 
-def fetch(pairs, sems):
-    copies = [pltpu.make_async_copy(src, dst, sems.at[i]) for i, (src, dst) in enumerate(pairs)]
+def spread_kernel(near_ref, extra_ref, out_ref):
+    for x in range(4):
+        out_ref[x] = near_ref[...]
+
+
+def scalars(pick_ref, put_ref, pick, put, sems):
+    copies = [pltpu.make_async_copy(pick_ref, pick, sems.at[0]), pltpu.make_async_copy(put_ref, put, sems.at[1])]
     for copy in copies:
         copy.start()
     return copies
 
 
-def tile_copy(tiles_ref, held, sems, step):
-    part = pl.ds(step * STEP, STEP)
-    return pltpu.make_async_copy(tiles_ref.at[part], held.at[part], sems.at[step])
-
-
-def forward_kernel(
-    count_ref, rows_ref, cols_ref, source_ref, extra_ref, tiles_ref, out_ref,
-    total, count, rows, cols, sems, held, tile_sems,
-):
+def forward_kernel(cols_ref, row_to_ref, source_ref, extra_ref, tiles_ref, out_ref, total, cols, row_to, sems):
     steps = tiles_ref.shape[0] // STEP
     blocks = total.shape[0] - 1
-    small = fetch([(count_ref, count), (rows_ref, rows), (cols_ref, cols)], sems)
-    for step in range(steps):
-        tile_copy(tiles_ref, held, tile_sems, step).start()
+    small = scalars(cols_ref, row_to_ref, cols, row_to, sems)
     total[...] = jnp.zeros_like(total)
     for copy in small:
         copy.wait()
-    live = count[0]
 
     @pl.loop(0, steps)
     def work(step):
-        tile_copy(tiles_ref, held, tile_sems, step).wait()
         products = []
         for j in range(STEP):
-            col = cols[step * STEP + j]
+            col = cols[0, step * STEP + j]
             lanes = pl.ds(pl.multiple_of((col % 2) * TILE, TILE), TILE)
             products.append(
                 lax.dot_general(
-                    source_ref[col // 2, :, lanes], held[step * STEP + j], NT, preferred_element_type=F32
+                    source_ref[col // 2, :, lanes], tiles_ref[step * STEP + j], NT, preferred_element_type=F32
                 )
             )
         for j in range(STEP):
-            slot = step * STEP + j
-            row = jnp.where(slot < live, rows[slot], blocks)
+            row = row_to[0, step * STEP + j]
             total[row] = total[row] + products[j]
 
     for d in range(blocks):
@@ -115,15 +111,9 @@
         out_ref[d, 64:80, :] = jnp.concatenate([part[0:16], part[16:32]], axis=1).astype(BF16)
 
 
-def backward_kernel(
-    count_ref, rows_ref, cols_ref, got_ref, tiles_ref, out_ref,
-    total, count, rows, cols, sems, held, tile_sems,
-):
+def backward_kernel(rows_ref, col_to_ref, got_ref, tiles_ref, out_ref, total, rows, col_to, sems):
     steps = tiles_ref.shape[0] // STEP
-    blocks = total.shape[0] - 1
-    small = fetch([(count_ref, count), (rows_ref, rows), (cols_ref, cols)], sems)
-    for step in range(steps):
-        tile_copy(tiles_ref, held, tile_sems, step).start()
+    small = scalars(rows_ref, col_to_ref, rows, col_to, sems)
     total[...] = jnp.zeros_like(total)
     grad_a = got_ref[0, 32:64, :].astype(F32)
     grad_b = got_ref[0, 64:80, :].astype(F32)
@@ -139,20 +129,17 @@
     )
     for copy in small:
         copy.wait()
-    live = count[0]
 
     @pl.loop(0, steps)
     def work(step):
-        tile_copy(tiles_ref, held, tile_sems, step).wait()
         products = []
         for j in range(STEP):
-            row = rows[step * STEP + j]
+            row = rows[0, step * STEP + j]
             products.append(
-                jnp.dot(got_ref[row, 0:32, :], held[step * STEP + j], preferred_element_type=F32)
+                jnp.dot(got_ref[row, 0:32, :], tiles_ref[step * STEP + j], preferred_element_type=F32)
             )
         for j in range(STEP):
-            slot = step * STEP + j
-            col = jnp.where(slot < live, cols[slot], blocks)
+            col = col_to[0, step * STEP + j]
             total[col] = total[col] + products[j]
 
     for x in range(4):
@@ -189,34 +176,39 @@
     far = pl.BlockSpec(memory_space=pltpu.MemorySpace.HBM)
     slots = tile_values.shape[0]
     scratch = [
-        pltpu.SMEM((1,), jnp.int32),
-        pltpu.SMEM((slots,), jnp.int32),
-        pltpu.SMEM((slots,), jnp.int32),
-        pltpu.SemaphoreType.DMA((3,)),
-        pltpu.VMEM(tile_values.shape, BF16),
-        pltpu.SemaphoreType.DMA((slots // STEP,)),
+        pltpu.SMEM((1, slots), jnp.int32),
+        pltpu.SMEM((1, slots), jnp.int32),
+        pltpu.SemaphoreType.DMA((2,)),
     ]
     params = pltpu.CompilerParams(vmem_limit_bytes=16 * 2**20)
-    tile_params = pltpu.CompilerParams(vmem_limit_bytes=51 * 2**20)
-    near = lax.all_gather(features, "zh", axis=0)
-    spread = jnp.broadcast_to(near[None], (4, *near.shape))
+    near = lax.all_to_all(jnp.broadcast_to(features[None], (4, *features.shape)), "zh", 0, 0, tiled=True)
+    rows = tile_rows.reshape(1, slots)
+    cols = tile_cols.reshape(1, slots)
+    extra, row_to, col_to = pl.pallas_call(
+        prepare_kernel,
+        in_specs=[pl.BlockSpec(memory_space=pltpu.MemorySpace.SMEM)] + [vmem] * 4,
+        out_specs=(vmem,) * 3,
+        out_shape=(shape((2, 16, TILE), BF16), shape(rows.shape, jnp.int32), shape(cols.shape, jnp.int32)),
+        compiler_params=params,
+        cost_estimate=pl.CostEstimate(flops=10**10, bytes_accessed=0, transcendentals=0),
+    )(tile_count, weight, labels.reshape(1, -1), rows, cols)
+    spread = pl.pallas_call(
+        spread_kernel,
+        in_specs=[vmem, far],
+        out_specs=vmem,
+        out_shape=shape((4, *near.shape), BF16),
+        compiler_params=params,
+        cost_estimate=pl.CostEstimate(flops=10**10, bytes_accessed=0, transcendentals=0),
+    )(near, extra)
     source = lax.all_to_all(spread, "x", 0, 0, tiled=True).reshape(16, *features.shape)
-    extra = pl.pallas_call(
-        prepare_kernel,
-        in_specs=[vmem, vmem],
-        out_specs=vmem,
-        out_shape=shape((2, 16, TILE), BF16),
-        compiler_params=params,
-        cost_estimate=pl.CostEstimate(flops=10**10, bytes_accessed=0, transcendentals=0),
-    )(weight, labels.reshape(1, -1))
     sent = pl.pallas_call(
         forward_kernel,
-        in_specs=[far, far, far, vmem, vmem, far],
+        in_specs=[far, far, vmem, vmem, vmem],
         out_specs=vmem,
         out_shape=shape((4, 8, 48, TILE), BF16),
         scratch_shapes=[pltpu.VMEM((9, 32, TILE), F32), *scratch],
-        compiler_params=tile_params,
-    )(tile_count, tile_rows, tile_cols, source, extra, tile_values)
+        compiler_params=params,
+    )(cols, row_to, source, extra, tile_values)
     got = lax.all_to_all(sent.reshape(32, 48, TILE), ("zl", "y", "core"), 0, 0, tiled=True)
     back = pl.pallas_call(
         middle_kernel,
@@ -225,16 +217,17 @@
         out_shape=shape((8, 80, TILE), BF16),
         scratch_shapes=[pltpu.VMEM((256, TILE), BF16)] * 3,
         compiler_params=params,
+        cost_estimate=pl.CostEstimate(flops=10**10, bytes_accessed=0, transcendentals=0),
     )(got)
     grads = lax.all_to_all(back, DEPTH, 0, 0, tiled=True)
     parts = pl.pallas_call(
         backward_kernel,
-        in_specs=[far, far, far, vmem, far],
+        in_specs=[far, far, vmem, vmem],
         out_specs=vmem,
         out_shape=shape((4, 152, 256), BF16),
         scratch_shapes=[pltpu.VMEM((33, 32, TILE), F32), *scratch],
-        compiler_params=tile_params,
-    )(tile_count, tile_rows, tile_cols, grads, tile_values)
+        compiler_params=params,
+    )(rows, col_to, grads, tile_values)
     lines = lax.all_to_all(parts, "x", 0, 0, tiled=True)
     summed = pl.pallas_call(
         sum_kernel,

time: 105 us -> 103 us (0.981); the launches traced: 105 us -> 102 us
  blocking collectives: 83.9 us -> 65.2 us
  starting transfers between devices: 4.29 us -> 14.2 us
  waiting for transfers between devices: 4.48 us -> 10.6 us
  Pallas kernels: 9.01 us -> 6.56 us
  local copies, waits for them, and re-layouts: 2.13 us -> 4.05 us
    all_gather x1 -> x0, blocking collectives: 25 us -> none  [body(): near = lax.all_gather(features, 'zh', axis=0)]
    all_to_all x0 -> x1, blocking collectives: none -> 11 us  [body(): lax.all_to_all(spread, 'x', 0, 0, tiled=True).reshape(16, *features.shape)]
    all_to_all x1, starting transfers between devices: 4.29 us -> 14.2 us  [body(): lax.all_to_all(jnp.broadcast_to(features[None], (4, *features.shape)), 'z...]
    all_to_all x1, waiting for transfers between devices: 4.48 us -> 10.6 us  [body(): lax.all_to_all(jnp.broadcast_to(features[None], (4, *features.shape)), 'z...]
    all_to_all x1, blocking collectives: 20.8 us -> 16.7 us  [body(): ours = lax.all_to_all(summed, 'zh', 0, 0, tiled=True)]
    pallas_call x3 -> x4, Pallas kernels: 7.7 us -> 5.25 us  [the longest x1 3.04 us: body(): pl.pallas_call(forward_kernel, in_specs=[far, far, vmem, vmem, vmem], out...]
    unnamed x8 -> x14, local copies, waits for them, and re-layouts: 1.4 us -> 2.71 us
where the time goes in v5:
time: 103 us; the launch traced here: 102 us
  blocking collectives  65.2 us (63%)
  starting transfers between devices  14.2 us (14%)
  waiting for transfers between devices  10.6 us (10%)
  Pallas kernels  6.56 us (6%)
  local copies, waits for them, and re-layouts  4.05 us (4%)
  between operations  1.32 us (1%)
    all_to_all x1, blocking collectives, body(): lax.all_to_all(sent.reshape(32, 48, TILE), ('zl', 'y', 'core'), 0, 0, til...  19.1 us
    all_to_all x1, blocking collectives, body(): ours = lax.all_to_all(summed, 'zh', 0, 0, tiled=True)  16.7 us
    all_to_all x1, starting transfers between devices, body(): lax.all_to_all(jnp.broadcast_to(features[None], (4, *features.shape)), 'z...  14.2 us
    all_to_all x1, blocking collectives, body(): lax.all_to_all(spread, 'x', 0, 0, tiled=True).reshape(16, *features.shape)  11 us
    all_to_all x1, waiting for transfers between devices, body(): lax.all_to_all(jnp.broadcast_to(features[None], (4, *features.shape)), 'z...  10.6 us
    all_to_all x1, blocking collectives, body(): lines = lax.all_to_all(parts, 'x', 0, 0, tiled=True)  9.61 us
    all_to_all x1, blocking collectives, body(): grads = lax.all_to_all(back, DEPTH, 0, 0, tiled=True)  8.88 us
    pallas_call x1, Pallas kernels, body(): pl.pallas_call(forward_kernel, in_specs=[far, far, vmem, vmem, vmem], out...  3.04 us
  transfers between devices with their start and end apart: 1, of which 1 were waited for; matrix products, arithmetic and copies ran while one was open for 0% of the time, Pallas kernels for 0%

profile of v5, /device:TPU:32, one launch (start us, length us, event | category | flops | bytes accessed | tf_op | source)
XLA Modules:
  0.0 101.9 jit_solution(110567110786658764)
XLA Ops:
  0.6 1.3 %broadcast_in_dim.2 = bf16[4,32,256]{2,1,0:T(8,128)(2,1)} broadcast(bf16[32,256]{1,0:T(8,128)(2,1)} %param.7), dimensions={1,2} | broadcast | bytes 81920 | tf_op jit(solution)/shard_map/broadcast_in_dim | solution.py:184
  2.0 14.2 %all-to-all-start = ((bf16[4,32,256]{2,1,0:T(8,128)(2,1)}), bf16[4,32,256]{2,1,0:T(8,128)(2,1)S(1)}, u32[]{:S(2)}, u32[]{:S(2)}) async-start(bf16[4,32,256]{2,1,0:T(8,128)(2,1)} %broadcast_in_dim.2), calls=%async_computation | async-start | bytes 131072 | tf_op jit(solution)/shard_map/all_to_all | solution.py:184
  16.8 0.0 copy-start.1
  16.8 0.6 copy-done.1
  17.5 0.0 copy-start.3
  17.5 0.7 copy-done.3
  18.1 0.0 copy-start.5
  18.1 0.7 copy-done.5
  18.8 0.0 copy-start.6
  18.8 0.7 copy-done.6
  19.5 0.1 shard_map.86
  19.7 10.6 %all-to-all-done.near_ref = bf16[4,32,256]{2,1,0:T(8,128)(2,1)S(1)} async-done(((bf16[4,32,256]{2,1,0:T(8,128)(2,1)}), bf16[4,32,256]{2,1,0:T(8,128)(2,1)S(1)}, u32[]{:S(2)}, u32[]{:S(2)}) %all-to-all-start) | async-done | bytes 65568 | tf_op jit(solution)/shard_map/all_to_all | solution.py:184
  30.2 0.0 copy-start
  30.2 0.0 copy-start.4
  30.2 11.0 %all_to_all.30 = bf16[4,4,32,256]{3,2,1,0:T(8,128)(2,1)S(1)} all-to-all(bf16[4,4,32,256]{3,2,1,0:T(8,128)(2,1)S(1)} %shard_map.87), channel_id=1, replica_groups=mesh['x'=4,'zh'=4,'zl'=4,'y'=4,'core'=2] {'x'}, dimensions={0} | all-to-all | bytes 524288 | tf_op jit(solution)/shard_map/all_to_all | solution.py:203
  41.3 0.0 copy-done
  41.3 0.0 copy-done.4
  41.3 3.0 %shard_map.88 = bf16[4,8,48,128]{3,2,1,0:T(8,128)(2,1)S(1)} custom-call(s32[1,128]{1,0:T(1,128)S(1)} %bitcast.10, s32[1,128]{1,0:T(1,128)S(1)} %get-tuple-element.6.row_to_ref, bf16[16,32,256]{2,1,0:T(8,128)(2,1)S(1)} %bitcast.6, bf16[2,16,128]{2,1,0:T(8,128)(2,1)S(1)} %get-tuple-element.7.extra_ref, bf16[128,128,128]{2,1,0:T(8,128)(2,1)S(1)} %copy-done), custom_call_target="tpu_custom_call" | custom-call | tf_op jit(solution)/shard_map/pallas_call | solution.py:204
  44.3 19.1 %all_to_all.31.got_ref = bf16[32,48,128]{2,1,0:T(8,128)(2,1)S(1)} all-to-all(bf16[32,48,128]{2,1,0:T(8,128)(2,1)S(1)} %bitcast.5), channel_id=1, replica_groups=mesh['x'=4,'zh'=4,'zl'=4,'y'=4,'core'=2] {'zl','y','core'}, dimensions={0} | all-to-all | bytes 786432 | tf_op jit(solution)/shard_map/all_to_all | solution.py:212
  63.4 0.0 copy-start.2
  63.4 0.6 shard_map.89
  64.0 8.9 %all_to_all.32.got_ref = bf16[8,80,128]{2,1,0:T(8,128)(2,1)S(1)} all-to-all(bf16[8,80,128]{2,1,0:T(8,128)(2,1)S(1)} %shard_map.89), channel_id=1, replica_groups=mesh['x'=4,'zh'=4,'zl'=4,'y'=4,'core'=2] {'y','core'}, dimensions={0} | all-to-all | bytes 327680 | tf_op jit(solution)/shard_map/all_to_all | solution.py:222
  72.8 0.0 copy-done.2
  72.9 2.0 %shard_map.90 = bf16[4,152,256]{2,1,0:T(8,128)(2,1)S(1)} custom-call(s32[1,128]{1,0:T(1,128)S(1)} %bitcast.8, s32[1,128]{1,0:T(1,128)S(1)} %get-tuple-element.5.col_to_ref, bf16[8,80,128]{2,1,0:T(8,128)(2,1)S(1)} %all_to_all.32.got_ref, bf16[128,128,128]{2,1,0:T(8,128)(2,1)S(1)} %copy-done), custom_call_target="tpu_custom_call" | custom-call | tf_op jit(solution)/shard_map/pallas_call | solution.py:223
  74.9 9.6 %all_to_all.33.got_ref = bf16[4,152,256]{2,1,0:T(8,128)(2,1)S(1)} all-to-all(bf16[4,152,256]{2,1,0:T(8,128)(2,1)S(1)} %shard_map.90), channel_id=1, replica_groups=mesh['x'=4,'zh'=4,'zl'=4,'y'=4,'core'=2] {'x'}, dimensions={0} | all-to-all | bytes 622592 | tf_op jit(solution)/shard_map/all_to_all | solution.py:231
  84.6 16.7 %all_to_all.34.got_ref = bf16[4,56,256]{2,1,0:T(8,128)(2,1)S(1)} all-to-all(bf16[4,56,256]{2,1,0:T(8,128)(2,1)S(1)} %shard_map.91), channel_id=1, replica_groups=mesh['x'=4,'zh'=4,'zl'=4,'y'=4,'core'=2] {'zh'}, dimensions={0} | all-to-all | bytes 229376 | tf_op jit(solution)/shard_map/all_to_all | solution.py:239
  101.2 0.7 shard_map.92
  (2 shorter events, 0.1 us)
Async XLA Ops:
  2.0 28.2 %all-to-all-start = ((bf16[4,32,256]{2,1,0:T(8,128)(2,1)}), bf16[4,32,256]{2,1,0:T(8,128)(2,1)S(1)}, u32[]{:S(2)}, u32[]{:S(2)}) async-start(bf16[4,32,256]{2,1,0:T(8,128)(2,1)} %broadcast_in_dim.2), calls=%async_computation | async-start | bytes 131072 | tf_op jit(solution)/shard_map/all_to_all | solution.py:184
  16.8 0.7 copy-start.1
  17.5 0.7 copy-start.3
  18.1 0.7 copy-start.5
  18.8 0.7 copy-start.6
  30.2 11.1 %copy-start = (bf16[128,128,128]{2,1,0:T(8,128)(2,1)S(1)}, bf16[128,128,128]{2,1,0:T(8,128)(2,1)}, u32[]{:S(2)}) copy-start(bf16[128,128,128]{2,1,0:T(8,128)(2,1)} %tiles_ref.3) | copy-start | bytes 12582916
  30.2 11.1 %copy-start.4 = (s32[128]{0:T(128)S(1)}, s32[128]{0:T(128)}, u32[]{:S(2)}) copy-start(s32[128]{0:T(128)} %param.11) | copy-start | bytes 1540
  63.4 9.5 %copy-start.2 = (s32[128]{0:T(128)S(1)}, s32[128]{0:T(128)}, u32[]{:S(2)}) copy-start(s32[128]{0:T(128)} %param.10) | copy-start | bytes 1540

commit v6 on v5

--- a/solution.py
+++ b/solution.py
@@ -16,46 +16,44 @@
 TN = (((0,), (0,)), ((), ()))
 
 
-def prepare_kernel(
-    count_ref, weight_ref, labels_ref, rows_ref, cols_ref, out_ref, row_to_ref, col_to_ref
-):
-    live = lax.broadcasted_iota(jnp.int32, rows_ref.shape, 1) < count_ref[0]
-    row_to_ref[...] = jnp.where(live, rows_ref[...], 8)
-    col_to_ref[...] = jnp.where(live, cols_ref[...], 32)
+def spread_kernel(count_ref, near_ref, out_ref, count_out_ref):
+    for x in range(4):
+        out_ref[x] = near_ref[...]
+    count_out_ref[...] = jnp.full(count_out_ref.shape, count_ref[0], jnp.int32)
+
+
+def scalars(refs, held, sems):
+    copies = [pltpu.make_async_copy(src, dst, sems.at[i]) for i, (src, dst) in enumerate(zip(refs, held))]
+    for copy in copies:
+        copy.start()
+    return copies
+
+
+def packed_rows(weight_ref, labels_ref, half):
     me = lax.axis_index("zl")
     weight = weight_ref[...].astype(F32)
     classes = weight.shape[1]
     mine = weight[0:8]
     for z in range(1, 4):
         mine = jnp.where(me == z, weight[8 * z : 8 * z + 8], mine)
-    labels = labels_ref[...].astype(F32)
+    labels = labels_ref[:, half * TILE : half * TILE + TILE].astype(F32)
     rest = jnp.concatenate([mine[:, TILE:], jnp.zeros((8, 64 - (classes - TILE)), F32)], axis=1)
-    for d in range(2):
-        half = labels[:, d * TILE : d * TILE + TILE]
-        both = jnp.concatenate([half[:, :64], half[:, 64:], jnp.zeros((6, 64), F32)], axis=0)
-        right = jnp.concatenate([rest, both], axis=1)
-        out_ref[d] = jnp.concatenate([mine[:, :TILE], right], axis=0).astype(BF16)
-
-
-def spread_kernel(near_ref, extra_ref, out_ref):
-    for x in range(4):
-        out_ref[x] = near_ref[...]
-
-
-def scalars(pick_ref, put_ref, pick, put, sems):
-    copies = [pltpu.make_async_copy(pick_ref, pick, sems.at[0]), pltpu.make_async_copy(put_ref, put, sems.at[1])]
-    for copy in copies:
-        copy.start()
-    return copies
-
-
-def forward_kernel(cols_ref, row_to_ref, source_ref, extra_ref, tiles_ref, out_ref, total, cols, row_to, sems):
+    both = jnp.concatenate([labels[:, :64], labels[:, 64:], jnp.zeros((6, 64), F32)], axis=0)
+    return jnp.concatenate([mine[:, :TILE], jnp.concatenate([rest, both], axis=1)], axis=0).astype(BF16)
+
+
+def forward_kernel(
+    count_ref, rows_ref, cols_ref, source_ref, weight_ref, labels_ref, tiles_ref, out_ref,
+    total, count, rows, cols, sems,
+):
     steps = tiles_ref.shape[0] // STEP
     blocks = total.shape[0] - 1
-    small = scalars(cols_ref, row_to_ref, cols, row_to, sems)
+    small = scalars((count_ref, rows_ref, cols_ref), (count, rows, cols), sems)
     total[...] = jnp.zeros_like(total)
+    extra = [packed_rows(weight_ref, labels_ref, half) for half in range(2)]
     for copy in small:
         copy.wait()
+    live = count[0, 0]
 
     @pl.loop(0, steps)
     def work(step):
@@ -69,11 +67,12 @@
                 )
             )
         for j in range(STEP):
-            row = row_to[0, step * STEP + j]
+            slot = step * STEP + j
+            row = jnp.where(slot < live, rows[0, slot], blocks)
             total[row] = total[row] + products[j]
 
     for d in range(blocks):
-        block = jnp.concatenate([total[d].astype(BF16), extra_ref[d % 2]], axis=0)
+        block = jnp.concatenate([total[d].astype(BF16), extra[d % 2]], axis=0)
         for z in range(4):
             out_ref[z, d] = block
 
@@ -111,9 +110,12 @@
         out_ref[d, 64:80, :] = jnp.concatenate([part[0:16], part[16:32]], axis=1).astype(BF16)
 
 
-def backward_kernel(rows_ref, col_to_ref, got_ref, tiles_ref, out_ref, total, rows, col_to, sems):
+def backward_kernel(
+    count_ref, rows_ref, cols_ref, got_ref, tiles_ref, out_ref, total, count, rows, cols, sems
+):
     steps = tiles_ref.shape[0] // STEP
-    small = scalars(rows_ref, col_to_ref, rows, col_to, sems)
+    blocks = total.shape[0] - 1
+    small = scalars((count_ref, rows_ref, cols_ref), (count, rows, cols), sems)
     total[...] = jnp.zeros_like(total)
     grad_a = got_ref[0, 32:64, :].astype(F32)
     grad_b = got_ref[0, 64:80, :].astype(F32)
@@ -130,6 +132,8 @@
     for copy in small:
         copy.wait()
 
+    live = count[0, 0]
+
     @pl.loop(0, steps)
     def work(step):
         products = []
@@ -139,7 +143,8 @@
                 jnp.dot(got_ref[row, 0:32, :], tiles_ref[step * STEP + j], preferred_element_type=F32)
             )
         for j in range(STEP):
-            col = col_to[0, step * STEP + j]
+            slot = step * STEP + j
+            col = jnp.where(slot < live, cols[0, slot], blocks)
             total[col] = total[col] + products[j]
 
     for x in range(4):
@@ -176,39 +181,32 @@
     far = pl.BlockSpec(memory_space=pltpu.MemorySpace.HBM)
     slots = tile_values.shape[0]
     scratch = [
+        pltpu.SMEM((1, TILE), jnp.int32),
         pltpu.SMEM((1, slots), jnp.int32),
         pltpu.SMEM((1, slots), jnp.int32),
-        pltpu.SemaphoreType.DMA((2,)),
+        pltpu.SemaphoreType.DMA((3,)),
     ]
     params = pltpu.CompilerParams(vmem_limit_bytes=16 * 2**20)
-    near = lax.all_to_all(jnp.broadcast_to(features[None], (4, *features.shape)), "zh", 0, 0, tiled=True)
     rows = tile_rows.reshape(1, slots)
     cols = tile_cols.reshape(1, slots)
-    extra, row_to, col_to = pl.pallas_call(
-        prepare_kernel,
-        in_specs=[pl.BlockSpec(memory_space=pltpu.MemorySpace.SMEM)] + [vmem] * 4,
-        out_specs=(vmem,) * 3,
-        out_shape=(shape((2, 16, TILE), BF16), shape(rows.shape, jnp.int32), shape(cols.shape, jnp.int32)),
+    near = lax.all_gather(features, "zh", axis=0)
+    spread, count = pl.pallas_call(
+        spread_kernel,
+        in_specs=[pl.BlockSpec(memory_space=pltpu.MemorySpace.SMEM), vmem],
+        out_specs=(vmem, vmem),
+        out_shape=(shape((4, *near.shape), BF16), shape((1, TILE), jnp.int32)),
         compiler_params=params,
         cost_estimate=pl.CostEstimate(flops=10**10, bytes_accessed=0, transcendentals=0),
-    )(tile_count, weight, labels.reshape(1, -1), rows, cols)
-    spread = pl.pallas_call(
-        spread_kernel,
-        in_specs=[vmem, far],
-        out_specs=vmem,
-        out_shape=shape((4, *near.shape), BF16),
-        compiler_params=params,
-        cost_estimate=pl.CostEstimate(flops=10**10, bytes_accessed=0, transcendentals=0),
-    )(near, extra)
+    )(tile_count, near)
     source = lax.all_to_all(spread, "x", 0, 0, tiled=True).reshape(16, *features.shape)
     sent = pl.pallas_call(
         forward_kernel,
-        in_specs=[far, far, vmem, vmem, vmem],
+        in_specs=[far, far, far, vmem, vmem, vmem, vmem],
         out_specs=vmem,
         out_shape=shape((4, 8, 48, TILE), BF16),
         scratch_shapes=[pltpu.VMEM((9, 32, TILE), F32), *scratch],
         compiler_params=params,
-    )(cols, row_to, source, extra, tile_values)
+    )(count, rows, cols, source, weight, labels.reshape(1, -1), tile_values)
     got = lax.all_to_all(sent.reshape(32, 48, TILE), ("zl", "y", "core"), 0, 0, tiled=True)
     back = pl.pallas_call(
         middle_kernel,
@@ -222,12 +220,12 @@
     grads = lax.all_to_all(back, DEPTH, 0, 0, tiled=True)
     parts = pl.pallas_call(
         backward_kernel,
-        in_specs=[far, far, vmem, vmem],
+        in_specs=[far, far, far, vmem, vmem],
         out_specs=vmem,
         out_shape=shape((4, 152, 256), BF16),
         scratch_shapes=[pltpu.VMEM((33, 32, TILE), F32), *scratch],
         compiler_params=params,
-    )(rows, col_to, grads, tile_values)
+    )(count, rows, cols, grads, tile_values)
     lines = lax.all_to_all(parts, "x", 0, 0, tiled=True)
     summed = pl.pallas_call(
         sum_kernel,

time: 103 us -> 103 us (level)
  blocking collectives: 65.2 us -> 94.8 us
  starting transfers between devices: 14.2 us -> 0 us
  waiting for transfers between devices: 10.6 us -> 0 us
  local copies, waits for them, and re-layouts: 4.05 us -> 0.02 us
    all_gather x0 -> x1, blocking collectives: none -> 25 us  [body(): near = lax.all_gather(features, 'zh', axis=0)]
    all_to_all x1 -> x0, starting transfers between devices: 14.2 us -> none  [body(): lax.all_to_all(jnp.broadcast_to(features[None], (4, *features.shape)), 'z...]
    all_to_all x1 -> x0, waiting for transfers between devices: 10.6 us -> none  [body(): lax.all_to_all(jnp.broadcast_to(features[None], (4, *features.shape)), 'z...]
    all_to_all x1, blocking collectives: 16.7 us -> 20.8 us  [body(): ours = lax.all_to_all(summed, 'zh', 0, 0, tiled=True)]
    unnamed x14 -> x10, local copies, waits for them, and re-layouts: 2.71 us -> 0.02 us
    broadcast_in_dim x1 -> x0, local copies, waits for them, and re-layouts: 1.34 us -> none  [body(): jnp.broadcast_to(features[None], (4, *features.shape))]
    pallas_call x4 -> x3, Pallas kernels: 5.25 us -> 5.13 us  [the longest x1 3.07 us: body(): pl.pallas_call(forward_kernel, in_specs=[far, far, far, vmem, vmem, vmem,...]
  transfers between devices with their start and end apart: 1 -> 0, of which waited for: 1 -> 0; matrix products, arithmetic and copies ran while one was open for 0% -> 0% of each run, Pallas kernels for 0% -> 0%
where the time goes in v6:
time: 103 us
  blocking collectives  94.8 us (92%)
  Pallas kernels  6.44 us (6%)
  between operations  1.35 us (1%)
    all_gather x1, blocking collectives, body(): near = lax.all_gather(features, 'zh', axis=0)  25 us
    all_to_all x1, blocking collectives, body(): ours = lax.all_to_all(summed, 'zh', 0, 0, tiled=True)  20.8 us
    all_to_all x1, blocking collectives, body(): lax.all_to_all(sent.reshape(32, 48, TILE), ('zl', 'y', 'core'), 0, 0, til...  19.5 us
    all_to_all x1, blocking collectives, body(): lax.all_to_all(spread, 'x', 0, 0, tiled=True).reshape(16, *features.shape)  11 us
    all_to_all x1, blocking collectives, body(): lines = lax.all_to_all(parts, 'x', 0, 0, tiled=True)  9.61 us
    all_to_all x1, blocking collectives, body(): grads = lax.all_to_all(back, DEPTH, 0, 0, tiled=True)  8.88 us
    pallas_call x1, Pallas kernels, body(): pl.pallas_call(forward_kernel, in_specs=[far, far, far, vmem, vmem, vmem,...  3.07 us

profile of v6, /device:TPU:32, one launch (start us, length us, event | category | flops | bytes accessed | tf_op | source)
XLA Modules:
  0.0 102.6 jit_solution(1127669515180106655)
XLA Ops:
  1.3 25.0 %all-gather = bf16[128,256]{1,0:T(8,128)(2,1)S(1)} all-gather(bf16[32,256]{1,0:T(8,128)(2,1)} %param.7), channel_id=2, replica_groups=mesh['x'=4,'zh'=4,'zl'=4,'y'=4,'core'=2] {'zh'}, dimensions={0}, use_global_device_ids=true | all-gather | bytes 81920 | tf_op jit(solution)/shard_map/all_gather | solution.py:192
  26.3 0.0 copy-start
  26.3 0.0 copy-start.1
  26.3 0.0 copy-start.2
  26.3 0.0 copy-start.3
  26.3 0.0 copy-start.4
  26.4 11.0 %all_to_all.25 = bf16[4,4,32,256]{3,2,1,0:T(8,128)(2,1)S(1)} all-to-all(bf16[4,4,32,256]{3,2,1,0:T(8,128)(2,1)S(1)} %get-tuple-element.5), channel_id=1, replica_groups=mesh['x'=4,'zh'=4,'zl'=4,'y'=4,'core'=2] {'x'}, dimensions={0} | all-to-all | bytes 524288 | tf_op jit(solution)/shard_map/all_to_all | solution.py:201
  37.4 0.0 copy-done
  37.4 0.0 copy-done.1
  37.4 0.0 copy-done.2
  37.4 0.0 copy-done.3
  37.4 0.0 copy-done.4
  37.4 3.1 %shard_map.87 = bf16[4,8,48,128]{3,2,1,0:T(8,128)(2,1)S(1)} custom-call(s32[1,128]{1,0:T(1,128)S(1)} %get-tuple-element.4.count_ref, s32[1,128]{1,0:T(1,128)S(1)} %bitcast.9, s32[1,128]{1,0:T(1,128)S(1)} %bitcast.11, bf16[16,32,256]{2,1,0:T(8,128)(2,1)S(1)} %bitcast.7, bf16[32,172]{1,0:T(8,128)(2,1)S(1)} %copy-done.1, s32[1,256]{1,0:T(1,128)S(1)} %bitcast.13, ...), custom_call_target="tpu_custom_call" | custom-call | tf_op jit(solution)/shard_map/pallas_call | solution.py:202
  40.5 19.5 %all_to_all.26.got_ref = bf16[32,48,128]{2,1,0:T(8,128)(2,1)S(1)} all-to-all(bf16[32,48,128]{2,1,0:T(8,128)(2,1)S(1)} %bitcast.6), channel_id=1, replica_groups=mesh['x'=4,'zh'=4,'zl'=4,'y'=4,'core'=2] {'zl','y','core'}, dimensions={0} | all-to-all | bytes 786432 | tf_op jit(solution)/shard_map/all_to_all | solution.py:210
  60.0 0.6 shard_map.88
  60.6 8.9 %all_to_all.27.got_ref = bf16[8,80,128]{2,1,0:T(8,128)(2,1)S(1)} all-to-all(bf16[8,80,128]{2,1,0:T(8,128)(2,1)S(1)} %shard_map.88), channel_id=1, replica_groups=mesh['x'=4,'zh'=4,'zl'=4,'y'=4,'core'=2] {'y','core'}, dimensions={0} | all-to-all | bytes 327680 | tf_op jit(solution)/shard_map/all_to_all | solution.py:220
  69.5 2.0 %shard_map.89 = bf16[4,152,256]{2,1,0:T(8,128)(2,1)S(1)} custom-call(s32[1,128]{1,0:T(1,128)S(1)} %get-tuple-element.4.count_ref, s32[1,128]{1,0:T(1,128)S(1)} %bitcast.10, s32[1,128]{1,0:T(1,128)S(1)} %bitcast.12, bf16[8,80,128]{2,1,0:T(8,128)(2,1)S(1)} %all_to_all.27.got_ref, bf16[128,128,128]{2,1,0:T(8,128)(2,1)S(1)} %copy-done), custom_call_target="tpu_custom_call" | custom-call | tf_op jit(solution)/shard_map/pallas_call | solution.py:221
  71.5 9.6 %all_to_all.28.got_ref = bf16[4,152,256]{2,1,0:T(8,128)(2,1)S(1)} all-to-all(bf16[4,152,256]{2,1,0:T(8,128)(2,1)S(1)} %shard_map.89), channel_id=1, replica_groups=mesh['x'=4,'zh'=4,'zl'=4,'y'=4,'core'=2] {'x'}, dimensions={0} | all-to-all | bytes 622592 | tf_op jit(solution)/shard_map/all_to_all | solution.py:229
  81.2 20.8 %all_to_all.29.got_ref = bf16[4,56,256]{2,1,0:T(8,128)(2,1)S(1)} all-to-all(bf16[4,56,256]{2,1,0:T(8,128)(2,1)S(1)} %shard_map.90), channel_id=1, replica_groups=mesh['x'=4,'zh'=4,'zl'=4,'y'=4,'core'=2] {'zh'}, dimensions={0} | all-to-all | bytes 229376 | tf_op jit(solution)/shard_map/all_to_all | solution.py:237
  102.0 0.7 shard_map.91
  (2 shorter events, 0.1 us)
Async XLA Ops:
  26.3 11.1 %copy-start = (bf16[128,128,128]{2,1,0:T(8,128)(2,1)S(1)}, bf16[128,128,128]{2,1,0:T(8,128)(2,1)}, u32[]{:S(2)}) copy-start(bf16[128,128,128]{2,1,0:T(8,128)(2,1)} %tiles_ref.3) | copy-start | bytes 12582916
  26.3 11.1 %copy-start.1 = (bf16[32,172]{1,0:T(8,128)(2,1)S(1)}, bf16[32,172]{1,0:T(8,128)(2,1)}, u32[]{:S(2)}) copy-start(bf16[32,172]{1,0:T(8,128)(2,1)} %weight_ref.1) | copy-start | bytes 33028
  26.3 11.1 %copy-start.2 = (s32[128]{0:T(128)S(1)}, s32[128]{0:T(128)}, u32[]{:S(2)}) copy-start(s32[128]{0:T(128)} %param.10) | copy-start | bytes 1540
  26.3 11.1 %copy-start.3 = (s32[128]{0:T(128)S(1)}, s32[128]{0:T(128)}, u32[]{:S(2)}) copy-start(s32[128]{0:T(128)} %param.11) | copy-start | bytes 1540
  26.3 11.1 %copy-start.4 = (s32[256]{0:T(256)S(1)}, s32[256]{0:T(256)}, u32[]{:S(2)}) copy-start(s32[256]{0:T(256)} %param.13) | copy-start | bytes 3076

commit v7 on v6

--- a/solution.py
+++ b/solution.py
@@ -46,7 +46,6 @@
     count_ref, rows_ref, cols_ref, source_ref, weight_ref, labels_ref, tiles_ref, out_ref,
     total, count, rows, cols, sems,
 ):
-    steps = tiles_ref.shape[0] // STEP
     blocks = total.shape[0] - 1
     small = scalars((count_ref, rows_ref, cols_ref), (count, rows, cols), sems)
     total[...] = jnp.zeros_like(total)
@@ -55,7 +54,7 @@
         copy.wait()
     live = count[0, 0]
 
-    @pl.loop(0, steps)
+    @pl.loop(0, (live + STEP - 1) // STEP)
     def work(step):
         products = []
         for j in range(STEP):
@@ -113,7 +112,6 @@
 def backward_kernel(
     count_ref, rows_ref, cols_ref, got_ref, tiles_ref, out_ref, total, count, rows, cols, sems
 ):
-    steps = tiles_ref.shape[0] // STEP
     blocks = total.shape[0] - 1
     small = scalars((count_ref, rows_ref, cols_ref), (count, rows, cols), sems)
     total[...] = jnp.zeros_like(total)
@@ -134,7 +132,7 @@
 
     live = count[0, 0]
 
-    @pl.loop(0, steps)
+    @pl.loop(0, (live + STEP - 1) // STEP)
     def work(step):
         products = []
         for j in range(STEP):

time: 103 us -> 102 us (level)
  the two profiles are of different devices: /device:TPU:32 before, /device:TPU:2 now
where the time goes in v7:
time: 102 us
  blocking collectives  95.7 us (94%)
  Pallas kernels  4.51 us (4%)
  between operations  1.35 us (1%)
    all_gather x1, blocking collectives, body(): near = lax.all_gather(features, 'zh', axis=0)  25.9 us
    all_to_all x1, blocking collectives, body(): ours = lax.all_to_all(summed, 'zh', 0, 0, tiled=True)  20.7 us
    all_to_all x1, blocking collectives, body(): lax.all_to_all(sent.reshape(32, 48, TILE), ('zl', 'y', 'core'), 0, 0, til...  19.5 us
    all_to_all x1, blocking collectives, body(): lines = lax.all_to_all(parts, 'x', 0, 0, tiled=True)  10.2 us
    all_to_all x1, blocking collectives, body(): lax.all_to_all(spread, 'x', 0, 0, tiled=True).reshape(16, *features.shape)  10.1 us
    all_to_all x1, blocking collectives, body(): grads = lax.all_to_all(back, DEPTH, 0, 0, tiled=True)  9.25 us

profile of v7, /device:TPU:2, one launch (start us, length us, event | category | flops | bytes accessed | tf_op | source)
XLA Modules:
  0.0 101.5 jit_solution(8724666810324073299)
XLA Ops:
  1.3 25.9 %all-gather = bf16[128,256]{1,0:T(8,128)(2,1)S(1)} all-gather(bf16[32,256]{1,0:T(8,128)(2,1)} %param.7), channel_id=2, replica_groups=mesh['x'=4,'zh'=4,'zl'=4,'y'=4,'core'=2] {'zh'}, dimensions={0}, use_global_device_ids=true | all-gather | bytes 81920 | tf_op jit(solution)/shard_map/all_gather | solution.py:190
  27.2 0.0 copy-start
  27.2 0.0 copy-start.1
  27.2 0.0 copy-start.2
  27.2 0.0 copy-start.3
  27.2 0.0 copy-start.4
  27.3 10.1 %all_to_all.25 = bf16[4,4,32,256]{3,2,1,0:T(8,128)(2,1)S(1)} all-to-all(bf16[4,4,32,256]{3,2,1,0:T(8,128)(2,1)S(1)} %get-tuple-element.5), channel_id=1, replica_groups=mesh['x'=4,'zh'=4,'zl'=4,'y'=4,'core'=2] {'x'}, dimensions={0} | all-to-all | bytes 524288 | tf_op jit(solution)/shard_map/all_to_all | solution.py:199
  37.4 0.0 copy-done
  37.4 0.0 copy-done.1
  37.4 0.0 copy-done.2
  37.4 0.0 copy-done.3
  37.4 0.0 copy-done.4
  37.4 1.9 %shard_map.87 = bf16[4,8,48,128]{3,2,1,0:T(8,128)(2,1)S(1)} custom-call(s32[1,128]{1,0:T(1,128)S(1)} %get-tuple-element.4.count_ref, s32[1,128]{1,0:T(1,128)S(1)} %bitcast.9, s32[1,128]{1,0:T(1,128)S(1)} %bitcast.11, bf16[16,32,256]{2,1,0:T(8,128)(2,1)S(1)} %bitcast.7, bf16[32,172]{1,0:T(8,128)(2,1)S(1)} %copy-done.1, s32[1,256]{1,0:T(1,128)S(1)} %bitcast.13, ...), custom_call_target="tpu_custom_call" | custom-call | tf_op jit(solution)/shard_map/pallas_call | solution.py:200
  39.3 19.5 %all_to_all.26.got_ref = bf16[32,48,128]{2,1,0:T(8,128)(2,1)S(1)} all-to-all(bf16[32,48,128]{2,1,0:T(8,128)(2,1)S(1)} %bitcast.6), channel_id=1, replica_groups=mesh['x'=4,'zh'=4,'zl'=4,'y'=4,'core'=2] {'zl','y','core'}, dimensions={0} | all-to-all | bytes 786432 | tf_op jit(solution)/shard_map/all_to_all | solution.py:208
  58.8 0.6 shard_map.88
  59.4 9.2 %all_to_all.27.got_ref = bf16[8,80,128]{2,1,0:T(8,128)(2,1)S(1)} all-to-all(bf16[8,80,128]{2,1,0:T(8,128)(2,1)S(1)} %shard_map.88), channel_id=1, replica_groups=mesh['x'=4,'zh'=4,'zl'=4,'y'=4,'core'=2] {'y','core'}, dimensions={0} | all-to-all | bytes 327680 | tf_op jit(solution)/shard_map/all_to_all | solution.py:218
  68.6 1.3 %shard_map.89 = bf16[4,152,256]{2,1,0:T(8,128)(2,1)S(1)} custom-call(s32[1,128]{1,0:T(1,128)S(1)} %get-tuple-element.4.count_ref, s32[1,128]{1,0:T(1,128)S(1)} %bitcast.10, s32[1,128]{1,0:T(1,128)S(1)} %bitcast.12, bf16[8,80,128]{2,1,0:T(8,128)(2,1)S(1)} %all_to_all.27.got_ref, bf16[128,128,128]{2,1,0:T(8,128)(2,1)S(1)} %copy-done), custom_call_target="tpu_custom_call" | custom-call | tf_op jit(solution)/shard_map/pallas_call | solution.py:219
  70.0 10.2 %all_to_all.28.got_ref = bf16[4,152,256]{2,1,0:T(8,128)(2,1)S(1)} all-to-all(bf16[4,152,256]{2,1,0:T(8,128)(2,1)S(1)} %shard_map.89), channel_id=1, replica_groups=mesh['x'=4,'zh'=4,'zl'=4,'y'=4,'core'=2] {'x'}, dimensions={0} | all-to-all | bytes 622592 | tf_op jit(solution)/shard_map/all_to_all | solution.py:227
  80.2 20.7 %all_to_all.29.got_ref = bf16[4,56,256]{2,1,0:T(8,128)(2,1)S(1)} all-to-all(bf16[4,56,256]{2,1,0:T(8,128)(2,1)S(1)} %shard_map.90), channel_id=1, replica_groups=mesh['x'=4,'zh'=4,'zl'=4,'y'=4,'core'=2] {'zh'}, dimensions={0} | all-to-all | bytes 229376 | tf_op jit(solution)/shard_map/all_to_all | solution.py:235
  100.9 0.7 shard_map.91
  (2 shorter events, 0.1 us)
Async XLA Ops:
  27.2 10.2 %copy-start = (bf16[128,128,128]{2,1,0:T(8,128)(2,1)S(1)}, bf16[128,128,128]{2,1,0:T(8,128)(2,1)}, u32[]{:S(2)}) copy-start(bf16[128,128,128]{2,1,0:T(8,128)(2,1)} %tiles_ref.3) | copy-start | bytes 12582916
  27.2 10.2 %copy-start.1 = (bf16[32,172]{1,0:T(8,128)(2,1)S(1)}, bf16[32,172]{1,0:T(8,128)(2,1)}, u32[]{:S(2)}) copy-start(bf16[32,172]{1,0:T(8,128)(2,1)} %weight_ref.1) | copy-start | bytes 33028
  27.2 10.2 %copy-start.2 = (s32[128]{0:T(128)S(1)}, s32[128]{0:T(128)}, u32[]{:S(2)}) copy-start(s32[128]{0:T(128)} %param.10) | copy-start | bytes 1540
  27.2 10.2 %copy-start.3 = (s32[128]{0:T(128)S(1)}, s32[128]{0:T(128)}, u32[]{:S(2)}) copy-start(s32[128]{0:T(128)} %param.11) | copy-start | bytes 1540
  27.2 10.2 %copy-start.4 = (s32[256]{0:T(256)S(1)}, s32[256]{0:T(256)}, u32[]{:S(2)}) copy-start(s32[256]{0:T(256)} %param.13) | copy-start | bytes 3076

commit v8 on v7

--- a/solution.py
+++ b/solution.py
@@ -16,10 +16,15 @@
 TN = (((0,), (0,)), ((), ()))
 
 
-def spread_kernel(count_ref, near_ref, out_ref, count_out_ref):
+def first_kernel(count_ref, own_ref, out_ref, count_out_ref):
+    for z in range(4):
+        out_ref[z] = own_ref[...]
+    count_out_ref[...] = jnp.full(count_out_ref.shape, count_ref[0], jnp.int32)
+
+
+def spread_kernel(near_ref, count_ref, out_ref):
     for x in range(4):
         out_ref[x] = near_ref[...]
-    count_out_ref[...] = jnp.full(count_out_ref.shape, count_ref[0], jnp.int32)
 
 
 def scalars(refs, held, sems):
@@ -187,15 +192,22 @@
     params = pltpu.CompilerParams(vmem_limit_bytes=16 * 2**20)
     rows = tile_rows.reshape(1, slots)
     cols = tile_cols.reshape(1, slots)
-    near = lax.all_gather(features, "zh", axis=0)
-    spread, count = pl.pallas_call(
-        spread_kernel,
+    four, count = pl.pallas_call(
+        first_kernel,
         in_specs=[pl.BlockSpec(memory_space=pltpu.MemorySpace.SMEM), vmem],
         out_specs=(vmem, vmem),
-        out_shape=(shape((4, *near.shape), BF16), shape((1, TILE), jnp.int32)),
+        out_shape=(shape((4, *features.shape), BF16), shape((1, TILE), jnp.int32)),
+        compiler_params=params,
+    )(tile_count, features)
+    near = lax.all_to_all(four, "zh", 0, 0, tiled=True)
+    spread = pl.pallas_call(
+        spread_kernel,
+        in_specs=[vmem, far],
+        out_specs=vmem,
+        out_shape=shape((4, *near.shape), BF16),
         compiler_params=params,
         cost_estimate=pl.CostEstimate(flops=10**10, bytes_accessed=0, transcendentals=0),
-    )(tile_count, near)
+    )(near, count)
     source = lax.all_to_all(spread, "x", 0, 0, tiled=True).reshape(16, *features.shape)
     sent = pl.pallas_call(
         forward_kernel,

time: 102 us -> 100 us (0.980)
  the two profiles are of different devices: /device:TPU:2 before, /device:TPU:32 now
where the time goes in v8:
time: 100 us
  blocking collectives  93.4 us (93%)
  Pallas kernels  4.57 us (5%)
  between operations  1.35 us (1%)
    all_to_all x1, blocking collectives, body(): near = lax.all_to_all(four, 'zh', 0, 0, tiled=True)  28 us
    all_to_all x1, blocking collectives, body(): lax.all_to_all(sent.reshape(32, 48, TILE), ('zl', 'y', 'core'), 0, 0, til...  19.1 us
    all_to_all x1, blocking collectives, body(): ours = lax.all_to_all(summed, 'zh', 0, 0, tiled=True)  16.7 us
    all_to_all x1, blocking collectives, body(): lax.all_to_all(spread, 'x', 0, 0, tiled=True).reshape(16, *features.shape)  11 us
    all_to_all x1, blocking collectives, body(): lines = lax.all_to_all(parts, 'x', 0, 0, tiled=True)  9.61 us
    all_to_all x1, blocking collectives, body(): grads = lax.all_to_all(back, DEPTH, 0, 0, tiled=True)  8.88 us

profile of v8, /device:TPU:32, one launch (start us, length us, event | category | flops | bytes accessed | tf_op | source)
XLA Modules:
  0.0 100.0 jit_solution(4197219423040536704)
XLA Ops:
  1.3 0.0 copy-start.2
  1.3 0.7 copy-done.2
  2.0 28.0 %all_to_all.30.near_ref = bf16[4,32,256]{2,1,0:T(8,128)(2,1)S(1)} all-to-all(bf16[4,32,256]{2,1,0:T(8,128)(2,1)S(1)} %get-tuple-element.5), channel_id=1, replica_groups=mesh['x'=4,'zh'=4,'zl'=4,'y'=4,'core'=2] {'zh'}, dimensions={0} | all-to-all | bytes 131072 | tf_op jit(solution)/shard_map/all_to_all | solution.py:202
  30.0 0.0 copy-start
  30.0 0.0 copy-start.1
  30.0 0.0 copy-start.3
  30.0 0.0 copy-start.4
  30.0 0.0 copy-start.5
  30.1 11.0 %all_to_all.31 = bf16[4,4,32,256]{3,2,1,0:T(8,128)(2,1)S(1)} all-to-all(bf16[4,4,32,256]{3,2,1,0:T(8,128)(2,1)S(1)} %shard_map.87), channel_id=1, replica_groups=mesh['x'=4,'zh'=4,'zl'=4,'y'=4,'core'=2] {'x'}, dimensions={0} | all-to-all | bytes 524288 | tf_op jit(solution)/shard_map/all_to_all | solution.py:211
  41.1 0.0 copy-done
  41.1 0.0 copy-done.1
  41.1 0.0 copy-done.3
  41.1 0.0 copy-done.4
  41.1 0.0 copy-done.5
  41.2 1.9 %shard_map.88 = bf16[4,8,48,128]{3,2,1,0:T(8,128)(2,1)S(1)} custom-call(s32[1,128]{1,0:T(1,128)S(1)} %get-tuple-element.4.count_ref, s32[1,128]{1,0:T(1,128)S(1)} %bitcast.7, s32[1,128]{1,0:T(1,128)S(1)} %bitcast.9, bf16[16,32,256]{2,1,0:T(8,128)(2,1)S(1)} %bitcast.6, bf16[32,172]{1,0:T(8,128)(2,1)S(1)} %copy-done.1, s32[1,256]{1,0:T(1,128)S(1)} %bitcast.11, ...), custom_call_target="tpu_custom_call" | custom-call | tf_op jit(solution)/shard_map/pallas_call | solution.py:212
  43.0 19.1 %all_to_all.32.got_ref = bf16[32,48,128]{2,1,0:T(8,128)(2,1)S(1)} all-to-all(bf16[32,48,128]{2,1,0:T(8,128)(2,1)S(1)} %bitcast.5), channel_id=1, replica_groups=mesh['x'=4,'zh'=4,'zl'=4,'y'=4,'core'=2] {'zl','y','core'}, dimensions={0} | all-to-all | bytes 786432 | tf_op jit(solution)/shard_map/all_to_all | solution.py:220
  62.1 0.6 shard_map.89
  62.7 8.9 %all_to_all.33.got_ref = bf16[8,80,128]{2,1,0:T(8,128)(2,1)S(1)} all-to-all(bf16[8,80,128]{2,1,0:T(8,128)(2,1)S(1)} %shard_map.89), channel_id=1, replica_groups=mesh['x'=4,'zh'=4,'zl'=4,'y'=4,'core'=2] {'y','core'}, dimensions={0} | all-to-all | bytes 327680 | tf_op jit(solution)/shard_map/all_to_all | solution.py:230
  71.5 1.4 %shard_map.90 = bf16[4,152,256]{2,1,0:T(8,128)(2,1)S(1)} custom-call(s32[1,128]{1,0:T(1,128)S(1)} %get-tuple-element.4.count_ref, s32[1,128]{1,0:T(1,128)S(1)} %bitcast.8, s32[1,128]{1,0:T(1,128)S(1)} %bitcast.10, bf16[8,80,128]{2,1,0:T(8,128)(2,1)S(1)} %all_to_all.33.got_ref, bf16[128,128,128]{2,1,0:T(8,128)(2,1)S(1)} %copy-done), custom_call_target="tpu_custom_call" | custom-call | tf_op jit(solution)/shard_map/pallas_call | solution.py:231
  72.9 9.6 %all_to_all.34.got_ref = bf16[4,152,256]{2,1,0:T(8,128)(2,1)S(1)} all-to-all(bf16[4,152,256]{2,1,0:T(8,128)(2,1)S(1)} %shard_map.90), channel_id=1, replica_groups=mesh['x'=4,'zh'=4,'zl'=4,'y'=4,'core'=2] {'x'}, dimensions={0} | all-to-all | bytes 622592 | tf_op jit(solution)/shard_map/all_to_all | solution.py:239
  82.6 16.7 %all_to_all.35.got_ref = bf16[4,56,256]{2,1,0:T(8,128)(2,1)S(1)} all-to-all(bf16[4,56,256]{2,1,0:T(8,128)(2,1)S(1)} %shard_map.91), channel_id=1, replica_groups=mesh['x'=4,'zh'=4,'zl'=4,'y'=4,'core'=2] {'zh'}, dimensions={0} | all-to-all | bytes 229376 | tf_op jit(solution)/shard_map/all_to_all | solution.py:247
  99.3 0.7 shard_map.92
  (3 shorter events, 0.1 us)
Async XLA Ops:
  1.3 0.7 copy-start.2
  30.0 11.1 %copy-start = (bf16[128,128,128]{2,1,0:T(8,128)(2,1)S(1)}, bf16[128,128,128]{2,1,0:T(8,128)(2,1)}, u32[]{:S(2)}) copy-start(bf16[128,128,128]{2,1,0:T(8,128)(2,1)} %tiles_ref.3) | copy-start | bytes 12582916
  30.0 11.1 %copy-start.1 = (bf16[32,172]{1,0:T(8,128)(2,1)S(1)}, bf16[32,172]{1,0:T(8,128)(2,1)}, u32[]{:S(2)}) copy-start(bf16[32,172]{1,0:T(8,128)(2,1)} %weight_ref.1) | copy-start | bytes 33028
  30.0 11.1 %copy-start.3 = (s32[128]{0:T(128)S(1)}, s32[128]{0:T(128)}, u32[]{:S(2)}) copy-start(s32[128]{0:T(128)} %param.10) | copy-start | bytes 1540
  30.0 11.1 %copy-start.4 = (s32[128]{0:T(128)S(1)}, s32[128]{0:T(128)}, u32[]{:S(2)}) copy-start(s32[128]{0:T(128)} %param.11) | copy-start | bytes 1540
  30.0 11.1 %copy-start.5 = (s32[256]{0:T(256)S(1)}, s32[256]{0:T(256)}, u32[]{:S(2)}) copy-start(s32[256]{0:T(256)} %param.13) | copy-start | bytes 3076

commit v9 on v8

--- a/solution.py
+++ b/solution.py
@@ -67,7 +67,7 @@
             lanes = pl.ds(pl.multiple_of((col % 2) * TILE, TILE), TILE)
             products.append(
                 lax.dot_general(
-                    source_ref[col // 2, :, lanes], tiles_ref[step * STEP + j], NT, preferred_element_type=F32
+                    tiles_ref[step * STEP + j], source_ref[col // 2, :, lanes], NT, preferred_element_type=F32
                 )
             )
         for j in range(STEP):
@@ -76,7 +76,7 @@
             total[row] = total[row] + products[j]
 
     for d in range(blocks):
-        block = jnp.concatenate([total[d].astype(BF16), extra[d % 2]], axis=0)
+        block = jnp.concatenate([total[d].T.astype(BF16), extra[d % 2]], axis=0)
         for z in range(4):
             out_ref[z, d] = block
 
@@ -214,7 +214,7 @@
         in_specs=[far, far, far, vmem, vmem, vmem, vmem],
         out_specs=vmem,
         out_shape=shape((4, 8, 48, TILE), BF16),
-        scratch_shapes=[pltpu.VMEM((9, 32, TILE), F32), *scratch],
+        scratch_shapes=[pltpu.VMEM((9, TILE, 32), F32), *scratch],
         compiler_params=params,
     )(count, rows, cols, source, weight, labels.reshape(1, -1), tile_values)
     got = lax.all_to_all(sent.reshape(32, 48, TILE), ("zl", "y", "core"), 0, 0, tiled=True)

time: 100 us -> 100 us (level)
  no operation moved by 1% of the time
where the time goes in v9:
time: 100 us; the launch traced here: 99.6 us
  blocking collectives  93.3 us (93%)
  Pallas kernels  4.21 us (4%)
  between operations  1.35 us (1%)
    all_to_all x1, blocking collectives, body(): near = lax.all_to_all(four, 'zh', 0, 0, tiled=True)  28 us
    all_to_all x1, blocking collectives, body(): lax.all_to_all(sent.reshape(32, 48, TILE), ('zl', 'y', 'core'), 0, 0, til...  19.1 us
    all_to_all x1, blocking collectives, body(): ours = lax.all_to_all(summed, 'zh', 0, 0, tiled=True)  16.7 us
    all_to_all x1, blocking collectives, body(): lax.all_to_all(spread, 'x', 0, 0, tiled=True).reshape(16, *features.shape)  11 us
    all_to_all x1, blocking collectives, body(): lines = lax.all_to_all(parts, 'x', 0, 0, tiled=True)  9.61 us
    all_to_all x1, blocking collectives, body(): grads = lax.all_to_all(back, DEPTH, 0, 0, tiled=True)  8.88 us

profile of v9, /device:TPU:32, one launch (start us, length us, event | category | flops | bytes accessed | tf_op | source)
XLA Modules:
  0.0 99.6 jit_solution(1273770892114986837)
XLA Ops:
  1.3 0.0 copy-start.2
  1.3 0.7 copy-done.2
  2.0 28.0 %all_to_all.30.near_ref = bf16[4,32,256]{2,1,0:T(8,128)(2,1)S(1)} all-to-all(bf16[4,32,256]{2,1,0:T(8,128)(2,1)S(1)} %get-tuple-element.5), channel_id=1, replica_groups=mesh['x'=4,'zh'=4,'zl'=4,'y'=4,'core'=2] {'zh'}, dimensions={0} | all-to-all | bytes 131072 | tf_op jit(solution)/shard_map/all_to_all | solution.py:202
  30.0 0.0 copy-start
  30.0 0.0 copy-start.1
  30.0 0.0 copy-start.3
  30.0 0.0 copy-start.4
  30.0 0.0 copy-start.5
  30.1 11.0 %all_to_all.31 = bf16[4,4,32,256]{3,2,1,0:T(8,128)(2,1)S(1)} all-to-all(bf16[4,4,32,256]{3,2,1,0:T(8,128)(2,1)S(1)} %shard_map.87), channel_id=1, replica_groups=mesh['x'=4,'zh'=4,'zl'=4,'y'=4,'core'=2] {'x'}, dimensions={0} | all-to-all | bytes 524288 | tf_op jit(solution)/shard_map/all_to_all | solution.py:211
  41.1 0.0 copy-done
  41.1 0.0 copy-done.1
  41.1 0.0 copy-done.3
  41.1 0.0 copy-done.4
  41.1 0.0 copy-done.5
  41.2 1.5 %shard_map.88 = bf16[4,8,48,128]{3,2,1,0:T(8,128)(2,1)S(1)} custom-call(s32[1,128]{1,0:T(1,128)S(1)} %get-tuple-element.4.count_ref, s32[1,128]{1,0:T(1,128)S(1)} %bitcast.7, s32[1,128]{1,0:T(1,128)S(1)} %bitcast.9, bf16[16,32,256]{2,1,0:T(8,128)(2,1)S(1)} %bitcast.6, bf16[32,172]{1,0:T(8,128)(2,1)S(1)} %copy-done.1, s32[1,256]{1,0:T(1,128)S(1)} %bitcast.11, ...), custom_call_target="tpu_custom_call" | custom-call | tf_op jit(solution)/shard_map/pallas_call | solution.py:212
  42.7 19.1 %all_to_all.32.got_ref = bf16[32,48,128]{2,1,0:T(8,128)(2,1)S(1)} all-to-all(bf16[32,48,128]{2,1,0:T(8,128)(2,1)S(1)} %bitcast.5), channel_id=1, replica_groups=mesh['x'=4,'zh'=4,'zl'=4,'y'=4,'core'=2] {'zl','y','core'}, dimensions={0} | all-to-all | bytes 786432 | tf_op jit(solution)/shard_map/all_to_all | solution.py:220
  61.7 0.6 shard_map.89
  62.3 8.9 %all_to_all.33.got_ref = bf16[8,80,128]{2,1,0:T(8,128)(2,1)S(1)} all-to-all(bf16[8,80,128]{2,1,0:T(8,128)(2,1)S(1)} %shard_map.89), channel_id=1, replica_groups=mesh['x'=4,'zh'=4,'zl'=4,'y'=4,'core'=2] {'y','core'}, dimensions={0} | all-to-all | bytes 327680 | tf_op jit(solution)/shard_map/all_to_all | solution.py:230
  71.2 1.4 %shard_map.90 = bf16[4,152,256]{2,1,0:T(8,128)(2,1)S(1)} custom-call(s32[1,128]{1,0:T(1,128)S(1)} %get-tuple-element.4.count_ref, s32[1,128]{1,0:T(1,128)S(1)} %bitcast.8, s32[1,128]{1,0:T(1,128)S(1)} %bitcast.10, bf16[8,80,128]{2,1,0:T(8,128)(2,1)S(1)} %all_to_all.33.got_ref, bf16[128,128,128]{2,1,0:T(8,128)(2,1)S(1)} %copy-done), custom_call_target="tpu_custom_call" | custom-call | tf_op jit(solution)/shard_map/pallas_call | solution.py:231
  72.6 9.6 %all_to_all.34.got_ref = bf16[4,152,256]{2,1,0:T(8,128)(2,1)S(1)} all-to-all(bf16[4,152,256]{2,1,0:T(8,128)(2,1)S(1)} %shard_map.90), channel_id=1, replica_groups=mesh['x'=4,'zh'=4,'zl'=4,'y'=4,'core'=2] {'x'}, dimensions={0} | all-to-all | bytes 622592 | tf_op jit(solution)/shard_map/all_to_all | solution.py:239
  82.2 16.7 %all_to_all.35.got_ref = bf16[4,56,256]{2,1,0:T(8,128)(2,1)S(1)} all-to-all(bf16[4,56,256]{2,1,0:T(8,128)(2,1)S(1)} %shard_map.91), channel_id=1, replica_groups=mesh['x'=4,'zh'=4,'zl'=4,'y'=4,'core'=2] {'zh'}, dimensions={0} | all-to-all | bytes 229376 | tf_op jit(solution)/shard_map/all_to_all | solution.py:247
  98.9 0.7 shard_map.92
  (3 shorter events, 0.1 us)
Async XLA Ops:
  1.3 0.7 copy-start.2
  30.0 11.1 %copy-start = (bf16[128,128,128]{2,1,0:T(8,128)(2,1)S(1)}, bf16[128,128,128]{2,1,0:T(8,128)(2,1)}, u32[]{:S(2)}) copy-start(bf16[128,128,128]{2,1,0:T(8,128)(2,1)} %tiles_ref.3) | copy-start | bytes 12582916
  30.0 11.1 %copy-start.1 = (bf16[32,172]{1,0:T(8,128)(2,1)S(1)}, bf16[32,172]{1,0:T(8,128)(2,1)}, u32[]{:S(2)}) copy-start(bf16[32,172]{1,0:T(8,128)(2,1)} %weight_ref.1) | copy-start | bytes 33028
  30.0 11.1 %copy-start.3 = (s32[128]{0:T(128)S(1)}, s32[128]{0:T(128)}, u32[]{:S(2)}) copy-start(s32[128]{0:T(128)} %param.10) | copy-start | bytes 1540
  30.0 11.1 %copy-start.4 = (s32[128]{0:T(128)S(1)}, s32[128]{0:T(128)}, u32[]{:S(2)}) copy-start(s32[128]{0:T(128)} %param.11) | copy-start | bytes 1540
  30.0 11.1 %copy-start.5 = (s32[256]{0:T(256)S(1)}, s32[256]{0:T(256)}, u32[]{:S(2)}) copy-start(s32[256]{0:T(256)} %param.13) | copy-start | bytes 3076

commit v10 on v7

--- a/solution.py
+++ b/solution.py
@@ -62,7 +62,7 @@
             lanes = pl.ds(pl.multiple_of((col % 2) * TILE, TILE), TILE)
             products.append(
                 lax.dot_general(
-                    source_ref[col // 2, :, lanes], tiles_ref[step * STEP + j], NT, preferred_element_type=F32
+                    tiles_ref[step * STEP + j], source_ref[col // 2, :, lanes], NT, preferred_element_type=F32
                 )
             )
         for j in range(STEP):
@@ -71,7 +71,7 @@
             total[row] = total[row] + products[j]
 
     for d in range(blocks):
-        block = jnp.concatenate([total[d].astype(BF16), extra[d % 2]], axis=0)
+        block = jnp.concatenate([total[d].T.astype(BF16), extra[d % 2]], axis=0)
         for z in range(4):
             out_ref[z, d] = block
 
@@ -202,7 +202,7 @@
         in_specs=[far, far, far, vmem, vmem, vmem, vmem],
         out_specs=vmem,
         out_shape=shape((4, 8, 48, TILE), BF16),
-        scratch_shapes=[pltpu.VMEM((9, 32, TILE), F32), *scratch],
+        scratch_shapes=[pltpu.VMEM((9, TILE, 32), F32), *scratch],
         compiler_params=params,
     )(count, rows, cols, source, weight, labels.reshape(1, -1), tile_values)
     got = lax.all_to_all(sent.reshape(32, 48, TILE), ("zl", "y", "core"), 0, 0, tiled=True)

time: 102 us -> 101 us (level)
  the two profiles are of different devices: /device:TPU:2 before, /device:TPU:32 now
where the time goes in v10:
time: 101 us
  blocking collectives  95 us (94%)
  Pallas kernels  4.18 us (4%)
  between operations  1.35 us (1%)
    all_gather x1, blocking collectives, body(): near = lax.all_gather(features, 'zh', axis=0)  25 us
    all_to_all x1, blocking collectives, body(): ours = lax.all_to_all(summed, 'zh', 0, 0, tiled=True)  21 us
    all_to_all x1, blocking collectives, body(): lax.all_to_all(sent.reshape(32, 48, TILE), ('zl', 'y', 'core'), 0, 0, til...  19.5 us
    all_to_all x1, blocking collectives, body(): lax.all_to_all(spread, 'x', 0, 0, tiled=True).reshape(16, *features.shape)  11 us
    all_to_all x1, blocking collectives, body(): lines = lax.all_to_all(parts, 'x', 0, 0, tiled=True)  9.64 us
    all_to_all x1, blocking collectives, body(): grads = lax.all_to_all(back, DEPTH, 0, 0, tiled=True)  8.88 us

profile of v10, /device:TPU:32, one launch (start us, length us, event | category | flops | bytes accessed | tf_op | source)
XLA Modules:
  0.0 100.6 jit_solution(14313083640500514079)
XLA Ops:
  1.3 25.0 %all-gather = bf16[128,256]{1,0:T(8,128)(2,1)S(1)} all-gather(bf16[32,256]{1,0:T(8,128)(2,1)} %param.7), channel_id=2, replica_groups=mesh['x'=4,'zh'=4,'zl'=4,'y'=4,'core'=2] {'zh'}, dimensions={0}, use_global_device_ids=true | all-gather | bytes 81920 | tf_op jit(solution)/shard_map/all_gather | solution.py:190
  26.3 0.0 copy-start
  26.3 0.0 copy-start.1
  26.3 0.0 copy-start.2
  26.3 0.0 copy-start.3
  26.3 0.0 copy-start.4
  26.4 11.0 %all_to_all.25 = bf16[4,4,32,256]{3,2,1,0:T(8,128)(2,1)S(1)} all-to-all(bf16[4,4,32,256]{3,2,1,0:T(8,128)(2,1)S(1)} %get-tuple-element.5), channel_id=1, replica_groups=mesh['x'=4,'zh'=4,'zl'=4,'y'=4,'core'=2] {'x'}, dimensions={0} | all-to-all | bytes 524288 | tf_op jit(solution)/shard_map/all_to_all | solution.py:199
  37.4 0.0 copy-done
  37.4 0.0 copy-done.1
  37.4 0.0 copy-done.2
  37.4 0.0 copy-done.3
  37.4 0.0 copy-done.4
  37.4 1.5 %shard_map.87 = bf16[4,8,48,128]{3,2,1,0:T(8,128)(2,1)S(1)} custom-call(s32[1,128]{1,0:T(1,128)S(1)} %get-tuple-element.4.count_ref, s32[1,128]{1,0:T(1,128)S(1)} %bitcast.9, s32[1,128]{1,0:T(1,128)S(1)} %bitcast.11, bf16[16,32,256]{2,1,0:T(8,128)(2,1)S(1)} %bitcast.7, bf16[32,172]{1,0:T(8,128)(2,1)S(1)} %copy-done.1, s32[1,256]{1,0:T(1,128)S(1)} %bitcast.13, ...), custom_call_target="tpu_custom_call" | custom-call | tf_op jit(solution)/shard_map/pallas_call | solution.py:200
  38.9 19.5 %all_to_all.26.got_ref = bf16[32,48,128]{2,1,0:T(8,128)(2,1)S(1)} all-to-all(bf16[32,48,128]{2,1,0:T(8,128)(2,1)S(1)} %bitcast.6), channel_id=1, replica_groups=mesh['x'=4,'zh'=4,'zl'=4,'y'=4,'core'=2] {'zl','y','core'}, dimensions={0} | all-to-all | bytes 786432 | tf_op jit(solution)/shard_map/all_to_all | solution.py:208
  58.5 0.6 shard_map.88
  59.0 8.9 %all_to_all.27.got_ref = bf16[8,80,128]{2,1,0:T(8,128)(2,1)S(1)} all-to-all(bf16[8,80,128]{2,1,0:T(8,128)(2,1)S(1)} %shard_map.88), channel_id=1, replica_groups=mesh['x'=4,'zh'=4,'zl'=4,'y'=4,'core'=2] {'y','core'}, dimensions={0} | all-to-all | bytes 327680 | tf_op jit(solution)/shard_map/all_to_all | solution.py:218
  67.9 1.3 %shard_map.89 = bf16[4,152,256]{2,1,0:T(8,128)(2,1)S(1)} custom-call(s32[1,128]{1,0:T(1,128)S(1)} %get-tuple-element.4.count_ref, s32[1,128]{1,0:T(1,128)S(1)} %bitcast.10, s32[1,128]{1,0:T(1,128)S(1)} %bitcast.12, bf16[8,80,128]{2,1,0:T(8,128)(2,1)S(1)} %all_to_all.27.got_ref, bf16[128,128,128]{2,1,0:T(8,128)(2,1)S(1)} %copy-done), custom_call_target="tpu_custom_call" | custom-call | tf_op jit(solution)/shard_map/pallas_call | solution.py:219
  69.3 9.6 %all_to_all.28.got_ref = bf16[4,152,256]{2,1,0:T(8,128)(2,1)S(1)} all-to-all(bf16[4,152,256]{2,1,0:T(8,128)(2,1)S(1)} %shard_map.89), channel_id=1, replica_groups=mesh['x'=4,'zh'=4,'zl'=4,'y'=4,'core'=2] {'x'}, dimensions={0} | all-to-all | bytes 622592 | tf_op jit(solution)/shard_map/all_to_all | solution.py:227
  79.0 21.0 %all_to_all.29.got_ref = bf16[4,56,256]{2,1,0:T(8,128)(2,1)S(1)} all-to-all(bf16[4,56,256]{2,1,0:T(8,128)(2,1)S(1)} %shard_map.90), channel_id=1, replica_groups=mesh['x'=4,'zh'=4,'zl'=4,'y'=4,'core'=2] {'zh'}, dimensions={0} | all-to-all | bytes 229376 | tf_op jit(solution)/shard_map/all_to_all | solution.py:235
  99.9 0.7 shard_map.91
  (2 shorter events, 0.1 us)
Async XLA Ops:
  26.3 11.1 %copy-start = (bf16[128,128,128]{2,1,0:T(8,128)(2,1)S(1)}, bf16[128,128,128]{2,1,0:T(8,128)(2,1)}, u32[]{:S(2)}) copy-start(bf16[128,128,128]{2,1,0:T(8,128)(2,1)} %tiles_ref.3) | copy-start | bytes 12582916
  26.3 11.1 %copy-start.1 = (bf16[32,172]{1,0:T(8,128)(2,1)S(1)}, bf16[32,172]{1,0:T(8,128)(2,1)}, u32[]{:S(2)}) copy-start(bf16[32,172]{1,0:T(8,128)(2,1)} %weight_ref.1) | copy-start | bytes 33028
  26.3 11.1 %copy-start.2 = (s32[128]{0:T(128)S(1)}, s32[128]{0:T(128)}, u32[]{:S(2)}) copy-start(s32[128]{0:T(128)} %param.10) | copy-start | bytes 1540
  26.3 11.1 %copy-start.3 = (s32[128]{0:T(128)S(1)}, s32[128]{0:T(128)}, u32[]{:S(2)}) copy-start(s32[128]{0:T(128)} %param.11) | copy-start | bytes 1540
  26.3 11.1 %copy-start.4 = (s32[256]{0:T(256)S(1)}, s32[256]{0:T(256)}, u32[]{:S(2)}) copy-start(s32[256]{0:T(256)} %param.13) | copy-start | bytes 3076
